TPU v7x, 512 devices: a whole 4x8x8 slice. The times are simulated.
512 devices in a mesh: blk: 128 (over y_lo, x, z, core), tile: 4 (over y_hi).
Axes of the slice: x: 4, y: 8 (y_hi: 4, y_lo: 2; y = y_hi * 2 + y_lo), z: 8, core: 2. Of those that a mesh axis runs over, the one named last changes fastest.
Arguments:
- right_side: float32 [512, 512], P('blk', 'tile'), may hold values from -6 to 6
- points: float32 [3, 512, 512], P(None, 'blk', 'tile'), may hold values from -5 to 5
- basis: float32 [512, 512, 256], P('blk', 'tile'), may hold values from -0.125 to 0.125
- skeleton: float32 [128, 3, 256], P('blk'), may hold values from -5 to 5
- cluster_sizes: int32 [512], P('blk'), may hold values from 256 to 512, as said below
- near_list: int32 [512, 4], P('blk'), may hold values from 0 to 511, as said below
- near_count: int32 [512], P('blk'), may hold values from 1 to 4, as said below
- far_mask: int32 [128, 128], P('blk'), may hold values from 0 to 1, as said below
Outputs:
- solution: float32 [512, 512], P('blk', 'tile')
- residual: float32 [512, 512], P('blk', 'tile')
Inputs may be any that keep to these rules, and one draw needn't show every extreme that they name: `cluster_sizes`: every leaf holds at least half of its slots live, and some leaf holds all 512. `near_list`: slot 0 names the leaf itself; every neighbour lies in the same subtree or in the subtree just before or after it in a closed loop of subtrees. `near_count`: some leaf uses all slots. `far_mask`: 0 or 1; 0 for a subtree with itself.
All inputs are finite; a program needn't handle non-finite values.
Results may differ from a plain program's by a relative error of at most 0.0003.
Values sent between devices are 32-bit elements; how exact they have to be, the bound alone decides.
A program may use at most 64 MiB of HBM per device.

v0:
```python
import math

import jax
import jax.numpy as jnp
from jax import lax
from jax.sharding import PartitionSpec as P

spread_sq = 0.25
exact_mode = lax.Precision.HIGHEST
norm_eps = 1e-06


def extended(block, sides, width):
    for axis, dim in sides:
        count = lax.axis_size(axis)
        forward = [(i, i + 1) for i in range(count - 1)]
        forward.append((count - 1, 0))
        backward = [(target, source) for source, target in forward]
        low = lax.ppermute(
            lax.slice_in_dim(block, block.shape[dim] - width, None, axis=dim), axis, forward
        )
        high = lax.ppermute(lax.slice_in_dim(block, 0, width, axis=dim), axis, backward)
        block = jnp.concatenate([low, block, high], axis=dim)
    return block


def coupling(targets, sources):
    dist_sq = jnp.sum((targets[:, :, None] - sources[:, None, :]) ** 2, axis=0)
    return 1.0 / jnp.sqrt(dist_sq + spread_sq)


def per_device(right_side, points, basis, skeleton, cluster_sizes, near_list, near_count, far_mask):
    leaf_dev, cols_dev = right_side.shape
    tile_count = lax.axis_size("tile")
    blk_count = lax.axis_size("blk")
    full_cols = cols_dev * tile_count
    rank = basis.shape[2]
    slot_count = near_list.shape[1]
    rank_dev = rank // tile_count
    tile_pos = lax.axis_index("tile")
    blk_pos = lax.axis_index("blk")
    near_scale = 2.0 / math.sqrt(full_cols * slot_count)
    far_scale = 4.0 / math.sqrt(rank * blk_count)
    positions = tile_pos * cols_dev + jnp.arange(cols_dev)
    live = (positions[None, :] < cluster_sizes[:, None]).astype(jnp.float32)
    pts_full = lax.all_gather(points, "tile", axis=2, tiled=True)
    pts_halo = extended(pts_full, (("blk", 1),), leaf_dev)
    relative = jnp.mod(near_list - blk_pos * leaf_dev + leaf_dev, blk_count * leaf_dev)
    slot_weight = (jnp.arange(slot_count)[None, :] < near_count[:, None]).astype(jnp.float32)
    far_row = far_mask[0].astype(jnp.float32)
    target_sky = lax.dynamic_slice_in_dim(skeleton[0], tile_pos * rank_dev, rank_dev, 1)

    def near_field(field):
        whole = lax.all_gather(field, "tile", axis=1, tiled=True)
        haloed = extended(whole, (("blk", 0),), leaf_dev)

        def block(leaf_id, slot_id):
            where_at = relative[leaf_id, slot_id]
            source_vals = lax.dynamic_index_in_dim(haloed, where_at, 0, keepdims=False)
            source_pts = lax.dynamic_index_in_dim(pts_halo, where_at, 1, keepdims=False)
            target_pts = lax.dynamic_index_in_dim(points, leaf_id, 1, keepdims=False)
            return jnp.dot(coupling(target_pts, source_pts), source_vals, precision=exact_mode)

        empty = jnp.zeros((leaf_dev, cols_dev), jnp.float32)

        def slot_step(running, flat_id):
            leaf_id = flat_id // slot_count
            slot_id = flat_id % slot_count
            value = block(leaf_id, slot_id) * slot_weight[leaf_id, slot_id]
            return (running.at[leaf_id].add(value), None)

        running, unused = lax.scan(slot_step, empty, jnp.arange(leaf_dev * slot_count))
        return running * near_scale

    def far_field(field):
        partial_coef = jnp.einsum("apk,ap->k", basis, field, precision=exact_mode)[None, :]
        coef = lax.psum(partial_coef, "tile")
        start_sky = jnp.zeros((rank_dev,), jnp.float32)
        coef_piece = lax.all_gather(coef, "blk", axis=0, tiled=True)
        pts_piece = lax.all_gather(skeleton, "blk", axis=0, tiled=True)

        def one_sub(number, running):
            weight = lax.dynamic_index_in_dim(far_row, number, 0, keepdims=False)
            return (
                running
                + jnp.dot(
                    coupling(target_sky, pts_piece[number]),
                    coef_piece[number],
                    precision=exact_mode,
                )
                * weight
            )

        sky_part = lax.fori_loop(0, coef_piece.shape[0], one_sub, start_sky)
        sky_all = lax.all_gather(sky_part * far_scale, "tile", axis=0, tiled=True)
        return jnp.einsum("apk,k->ap", basis, sky_all, precision=exact_mode)

    def apply_op(field):
        return live * (field + near_field(field) + far_field(field))

    start_vec = live * right_side
    beta = jnp.sqrt(lax.psum(jnp.sum(start_vec * start_vec), ("blk", "tile")) + norm_eps)
    first = start_vec / beta
    w_one = apply_op(first)
    h11 = lax.psum(jnp.sum(first * w_one), ("blk", "tile"))
    update = w_one - h11 * first
    h21 = jnp.sqrt(lax.psum(jnp.sum(update * update), ("blk", "tile")) + norm_eps)
    second = update / h21
    w_two = apply_op(second)
    h12 = lax.psum(jnp.sum(first * w_two), ("blk", "tile"))
    h22 = lax.psum(jnp.sum(second * (w_two - h12 * first)), ("blk", "tile"))
    rest = w_two - h12 * first - h22 * second
    h32 = jnp.sqrt(lax.psum(jnp.sum(rest * rest), ("blk", "tile")) + norm_eps)
    m_aa = h11 * h11 + h21 * h21
    m_ab = h11 * h12 + h21 * h22
    m_bb = h12 * h12 + h22 * h22 + h32 * h32
    determ = m_aa * m_bb - m_ab * m_ab
    y_one = beta * (m_bb * h11 - m_ab * h12) / determ
    y_two = beta * (m_aa * h12 - m_ab * h11) / determ
    solution = y_one * first + y_two * second
    residual = start_vec - y_one * w_one - y_two * w_two
    return (solution, residual)


def solution(mesh):
    placed = (
        P("blk", "tile"),
        P(None, "blk", "tile"),
        P("blk", "tile", None),
        P("blk", None, None),
        P("blk"),
        P("blk", None),
        P("blk"),
        P("blk", None),
    )
    return jax.shard_map(
        per_device,
        mesh=mesh,
        in_specs=placed,
        out_specs=(P("blk", "tile"), P("blk", "tile")),
        check_vma=False,
    )
```

profile of v0, /device:TPU:1, one launch (start us, length us, event | category | flops | bytes accessed | tf_op | source)
XLA Modules:
  0.0 1837.6 jit_solution(3732367363279674485)
XLA Ops:
  1.4 13.9 all_gather.25
  15.3 7.4 collective-permute-start
  24.0 1.9 collective-permute-start.1
  26.0 101.6 %psum.56 = f32[]{:T(128)} all-reduce(f32[]{:T(128)} %multiply_reduce_fusion.9), channel_id=1, replica_groups=mesh['blk'=128,'tile'=4] {'blk','tile'}, use_global_device_ids=true, to_apply=%region_1.2 | all-reduce | flops 1 | bytes 8 | tf_op jit(solution)/shard_map/psum | solution.py:102
  128.3 10.5 all_gather.26
  138.8 5.5 collective-permute-start.3
  144.3 1.9 collective-permute-start.2
  147.0 154.1 %all_gather.27 = f32[128,3,256]{2,1,0:T(4,128)S(1)} all-gather(f32[1,3,256]{2,1,0:T(4,128)S(1)} %copy.14), channel_id=1, replica_groups=mesh['blk'=128,'tile'=4] {'blk'}, dimensions={0}, use_global_device_ids=true | all-gather | bytes 396288 | tf_op jit(solution)/shard_map/all_gather | solution.py:80
  301.4 7.3 psum.57
  308.7 153.2 %all-gather = f32[128,1,256]{2,1,0:T(1,128)S(1)} all-gather(f32[1,1,256]{2,1,0:T(1,128)S(1)} %bitcast.183), channel_id=1, replica_groups=mesh['blk'=128,'tile'=4] {'blk'}, dimensions={0}, use_global_device_ids=true | all-gather | bytes 132096 | tf_op jit(solution)/shard_map/all_gather | solution.py:79
  462.5 196.0 %while.56 = (s32[]{:T(128)}, f32[64]{0:T(128)S(1)}, f32[3,64]{1,0:T(4,128)S(1)}, f32[128,3,256]{2,1,0:T(4,128)S(1)}, f32[128,256]{1,0:T(8,128)S(1)}, /*index=5*/f32[128]{0:T(128)S(1)}, s32[]{:T(128)}, s32[]{:T(128)}) while((s32[]{:T(128)}, f32[64]{0:T(128)S(1)}, f32[3,64]{1,0:T(4,128)S(1)}, f32[128,3,256]{2,1,0:T(4,128)S(1)}, ...), condition=%wide.region_9.10_spmd.clone, body=%wide.region_7.9_spmd.clone.sunk | while | flops 344259 | bytes 142975 | solution.py:94
  464.7 0.8 fusion.73
  466.3 0.8 fusion.73
  658.5 1.3 dynamic-slice.27
  660.6 9.3 all-reduce
  672.6 140.7 %while.54 = (s32[]{:T(128)}, f32[4,128]{1,0:T(4,128)S(1)}, s32[16]{0:T(128)S(1)}, f32[3,4,128]{2,0,1:T(4,128)S(1)}, s32[4,4]{1,0:T(4,128)S(1)}, /*index=5*/f32[3...) while((s32[]{:T(128)}, f32[4,128]{1,0:T(4,128)S(1)}, ...), condition=%wide.region_5.6_spmd, body=%wide.region_2.5_spmd.sunk | while | flops 1376679 | bytes 551956 | solution.py:72
  679.8 1.5 fusion.67
  688.6 1.5 fusion.67
  697.4 1.5 fusion.67
  706.2 1.5 fusion.67
  715.0 1.5 fusion.67
  723.8 1.5 fusion.67
  732.6 1.5 fusion.67
  741.4 1.5 fusion.67
  750.2 1.5 fusion.67
  759.0 1.5 fusion.67
  767.8 1.5 fusion.67
  776.6 1.5 fusion.67
  785.4 1.5 fusion.67
  794.2 1.5 fusion.67
  803.0 1.5 fusion.67
  811.8 1.5 fusion.67
  814.0 95.7 %psum.58 = f32[]{:T(128)} all-reduce(f32[]{:T(128)} %get-tuple-element.572), channel_id=1, replica_groups=mesh['blk'=128,'tile'=4] {'blk','tile'}, use_global_device_ids=true, to_apply=%region_11.12 | all-reduce | flops 1 | bytes 8 | tf_op jit(solution)/shard_map/psum | solution.py:105
  909.7 1.4 multiply_reduce_fusion.7
  911.1 94.4 %psum.59 = f32[]{:T(128)} all-reduce(f32[]{:T(128)} %multiply_reduce_fusion.7), channel_id=1, replica_groups=mesh['blk'=128,'tile'=4] {'blk','tile'}, use_global_device_ids=true, to_apply=%region_13.14 | all-reduce | flops 1 | bytes 8 | tf_op jit(solution)/shard_map/psum | solution.py:107
  1006.9 11.2 all_gather.30
  1018.1 5.5 collective-permute-start.5
  1023.6 3.1 collective-permute-start.4
  1026.9 6.9 psum.60
  1033.9 153.7 %all-gather.1 = f32[128,1,256]{2,1,0:T(1,128)S(1)} all-gather(f32[1,1,256]{2,1,0:T(1,128)S(1)} %bitcast.185), channel_id=1, replica_groups=mesh['blk'=128,'tile'=4] {'blk'}, dimensions={0}, use_global_device_ids=true | all-gather | bytes 132096 | tf_op jit(solution)/shard_map/all_gather | solution.py:79
  1187.6 197.9 %while.57 = (s32[]{:T(128)}, f32[64]{0:T(128)S(1)}, f32[3,64]{1,0:T(4,128)S(1)}, f32[128,3,256]{2,1,0:T(4,128)S(1)}, f32[128,256]{1,0:T(8,128)S(1)}, /*index=5*/f32[128]{0:T(128)S(1)}, s32[]{:T(128)}, s32[]{:T(128)}) while((s32[]{:T(128)}, f32[64]{0:T(128)S(1)}, f32[3,64]{1,0:T(4,128)S(1)}, f32[128,3,256]{2,1,0:T(4,128)S(1)}, ...), condition=%wide.region_21.22_spmd.clone, body=%wide.region_19.21_spmd.clone.sunk | while | flops 344259 | bytes 142975 | solution.py:94
  1385.6 9.3 all-reduce.1
  1396.9 142.4 %while.55 = (s32[]{:T(128)}, f32[4,128]{1,0:T(4,128)S(1)}, s32[16]{0:T(128)S(1)}, f32[3,4,128]{2,0,1:T(4,128)S(1)}, s32[4,4]{1,0:T(4,128)S(1)}, /*index=5*/f32[3...) while((s32[]{:T(128)}, f32[4,128]{1,0:T(4,128)S(1)}, ...), condition=%wide.region_17.18_spmd, body=%wide.region_14.17_spmd.sunk | while | flops 1376679 | bytes 551956 | solution.py:72
  1404.1 1.6 fusion.70
  1413.0 1.6 fusion.70
  1421.9 1.6 fusion.70
  1430.8 1.6 fusion.70
  1439.7 1.6 fusion.70
  1448.7 1.6 fusion.70
  1457.6 1.6 fusion.70
  1466.5 1.6 fusion.70
  1475.4 1.6 fusion.70
  1484.3 1.6 fusion.70
  1493.2 1.6 fusion.70
  1502.1 1.6 fusion.70
  1511.0 1.6 fusion.70
  1519.9 1.6 fusion.70
  1528.8 1.6 fusion.70
  1537.7 1.6 fusion.70
  1540.0 96.7 %psum.61 = f32[]{:T(128)} all-reduce(f32[]{:T(128)} %get-tuple-element.570), channel_id=1, replica_groups=mesh['blk'=128,'tile'=4] {'blk','tile'}, use_global_device_ids=true, to_apply=%region_23.24 | all-reduce | flops 1 | bytes 8 | tf_op jit(solution)/shard_map/psum | solution.py:110
  1638.0 1.3 multiply_reduce_fusion.5
  1640.6 94.8 %psum.62 = f32[]{:T(128)} all-reduce(f32[]{:T(128)} %multiply_reduce_fusion.5), channel_id=1, replica_groups=mesh['blk'=128,'tile'=4] {'blk','tile'}, use_global_device_ids=true, to_apply=%region_25.26 | all-reduce | flops 1 | bytes 8 | tf_op jit(solution)/shard_map/psum | solution.py:111
  1737.3 2.0 multiply_reduce_fusion.4
  1740.6 94.2 %psum.63 = f32[]{:T(128)} all-reduce(f32[]{:T(128)} %multiply_reduce_fusion.4), channel_id=1, replica_groups=mesh['blk'=128,'tile'=4] {'blk','tile'}, use_global_device_ids=true, to_apply=%region_27.28 | all-reduce | flops 1 | bytes 8 | tf_op jit(solution)/shard_map/psum | solution.py:113
  (1335 shorter events, 487.2 us)
Async XLA Ops:
  0.6 300.5 %copy-start = (f32[4,128,256]{2,1,0:T(8,128)S(1)}, f32[4,128,256]{2,1,0:T(8,128)}, u32[]{:S(2)}) copy-start(f32[4,128,256]{2,1,0:T(8,128)} %param.22) | copy-start | bytes 1572868
  15.3 656.6 %collective-permute-start = (f32[3,4,512]{2,0,1:T(4,128)S(1)}, f32[3,4,512]{2,0,1:T(4,128)S(1)}, u32[]{:S(2)}, u32[]{:S(2)}) collective-permute-start(f32[3,4,512]{2,0,1:T(4,128)S(1)} %all_gather.25), channel_id=1, source_target_pairs={{0,4},{4,8},{8,12},{12,16},{16,20},{20,24},{24,28},{28,32},{32,36}... | collective-permute-start | bytes 73736 | tf_op jit(solution)/shard_map/ppermute | solution.py:19
  22.7 0.7 copy-start.1
  22.7 0.7 copy-start.3
  24.0 647.8 %collective-permute-start.1 = (f32[3,4,512]{2,0,1:T(4,128)S(1)}, f32[3,4,512]{2,0,1:T(4,128)S(1)}, u32[]{:S(2)}, u32[]{:S(2)}) collective-permute-start(f32[3,4,512]{2,0,1:T(4,128)S(1)} %all_gather.25), channel_id=1, source_target_pairs={{4,0},{8,4},{12,8},{16,12},{20,16},{24,20},{28,24},{32,28},{36,32}... | collective-permute-start | bytes 73736 | tf_op jit(solution)/shard_map/ppermute | solution.py:22
  138.8 533.0 %collective-permute-start.3 = (f32[4,512]{1,0:T(4,128)S(1)}, f32[4,512]{1,0:T(4,128)S(1)}, u32[]{:S(2)}, u32[]{:S(2)}) collective-permute-start(f32[4,512]{1,0:T(4,128)S(1)} %all_gather.26), channel_id=1, source_target_pairs={{4,0},{8,4},{12,8},{16,12},{20,16},{24,20},{28,24},{32,28},{36,32}... | collective-permute-start | bytes 24584 | tf_op jit(solution)/shard_map/ppermute | solution.py:22
  144.3 527.6 %collective-permute-start.2 = (f32[4,512]{1,0:T(4,128)S(1)}, f32[4,512]{1,0:T(4,128)S(1)}, u32[]{:S(2)}, u32[]{:S(2)}) collective-permute-start(f32[4,512]{1,0:T(4,128)S(1)} %all_gather.26), channel_id=1, source_target_pairs={{0,4},{4,8},{8,12},{12,16},{16,20},{20,24},{24,28},{28,32},{32,36}... | collective-permute-start | bytes 24584 | tf_op jit(solution)/shard_map/ppermute | solution.py:19
  146.2 0.7 copy-start.4
  461.9 0.7 copy-start.7
  670.4 0.7 copy-start.5
  671.1 0.7 copy-start.6
  671.9 0.7 copy-start.2
  1018.1 378.7 %collective-permute-start.5 = (f32[4,512]{1,0:T(4,128)S(1)}, f32[4,512]{1,0:T(4,128)S(1)}, u32[]{:S(2)}, u32[]{:S(2)}) collective-permute-start(f32[4,512]{1,0:T(4,128)S(1)} %all_gather.30), channel_id=1, source_target_pairs={{4,0},{8,4},{12,8},{16,12},{20,16},{24,20},{28,24},{32,28},{36,32}... | collective-permute-start | bytes 24584 | tf_op jit(solution)/shard_map/ppermute | solution.py:22
  1023.6 373.2 %collective-permute-start.4 = (f32[4,512]{1,0:T(4,128)S(1)}, f32[4,512]{1,0:T(4,128)S(1)}, u32[]{:S(2)}, u32[]{:S(2)}) collective-permute-start(f32[4,512]{1,0:T(4,128)S(1)} %all_gather.30), channel_id=1, source_target_pairs={{0,4},{4,8},{8,12},{12,16},{16,20},{20,24},{24,28},{28,32},{32,36}... | collective-permute-start | bytes 24584 | tf_op jit(solution)/shard_map/ppermute | solution.py:19
where the time goes:
time: 1850 us; the launch traced here: 1840 us
  blocking collectives  1110 us (60%)
  matrix products  255 us (14%)
  local copies, waits for them, and re-layouts  221 us (12%)
  loops' own time  150 us (8%)
  other arithmetic  67.1 us (4%)
  starting transfers between devices  25.2 us (1%)
    all_gather x2, blocking collectives, far_field(): coef_piece = lax.all_gather(coef, 'blk', axis=0, tiled=True)  307 us
    dot_general x256, matrix products, one_sub(): jnp.dot(coupling(target_sky, pts_piece[number]), coef_piece[number], prec...  205 us
    all_gather x1, blocking collectives, far_field(): pts_piece = lax.all_gather(skeleton, 'blk', axis=0, tiled=True)  154 us
    dynamic_slice x256, local copies, waits for them, and re-layouts, one_sub(): weight = lax.dynamic_index_in_dim(far_row, number, 0, keepdims=False)  153 us
    another operation x2, loops' own time, near_field(): lax.scan(slot_step, empty, jnp.arange(leaf_dev * slot_count))  146 us
    psum x1, blocking collectives, per_device(): lax.psum(jnp.sum(start_vec * start_vec), ('blk', 'tile')) + norm_eps  102 us
    psum x1, blocking collectives, per_device(): h12 = lax.psum(jnp.sum(first * w_two), ('blk', 'tile'))  96.7 us
    psum x1, blocking collectives, per_device(): h11 = lax.psum(jnp.sum(first * w_one), ('blk', 'tile'))  95.7 us
  transfers between devices with their start and end apart: 6, of which 0 were waited for; matrix products, arithmetic and copies ran while one was open for 21% of the time, Pallas kernels for 0%

commit v1 on v0

v1 whole, which is shorter than its diff:
```python
import functools
import math

import jax
import jax.numpy as jnp
from jax import lax
from jax.experimental import pallas as pl
from jax.experimental.pallas import tpu as pltpu
from jax.sharding import PartitionSpec as P

MESH = pl.DeviceIdType.MESH
f32 = jnp.float32
spread_sq = 0.25
norm_eps = 1e-06

HALO_ONE, HALO_TWO, COEF_ONE, COEF_TWO, SKEL, FAR_ONE, FAR_TWO, SKY_ONE, SKY_TWO, SUM_TILE, SUM_BLK = range(11)
EXCHANGES = 11


def hops(step):
    dx, dyl, dz, dc = step
    return min(dx, 4 - dx) + dyl + min(dz, 8 - dz)


OTHERS = sorted(
    [(dx, dyl, dz, dc) for dx in range(4) for dyl in range(2) for dz in range(8) for dc in range(2) if dx or dyl or dz or dc],
    key=lambda step: -hops(step),
)


def kernel(
    rs_ref, pts_ref, basis_ref, skel_ref, sizes_ref, near_ref, count_ref, mask_ref,
    sol_ref, res_ref,
    hal1, hal2, abuf, skb, cbuf, pbuf, rtile, rblk,
    gfar, gnear, tfar, tnear, fcol, live_col, acc_near,
    ssem, rsem,
):
    g = lax.axis_index("blk")
    t = lax.axis_index("tile")
    near_scale = 2.0 / math.sqrt(512 * 4)
    far_scale = 4.0 / math.sqrt(256 * 128)

    core, z, x, yl = lax.rem(g, 2), lax.rem(g // 2, 8), lax.rem(g // 16, 4), g // 64
    low = {(dz, dc): lax.rem(z + dz, 8) * 2 + lax.rem(core + dc, 2) for dz in range(8) for dc in range(2)}
    high = {(dx, dy): lax.rem(yl + dy, 2) * 64 + lax.rem(x + dx, 4) * 16 for dx in range(4) for dy in range(2)}
    others = [high[s[0], s[1]] + low[s[2], s[3]] for s in OTHERS]
    tiles = [lax.rem(t + d, 4) for d in (2, 1, 3)]
    left, right = lax.rem(g + 127, 128), lax.rem(g + 1, 128)

    barrier = pltpu.get_barrier_semaphore()
    for tt in tiles:
        for gg in (left, right, g):
            pl.semaphore_signal(barrier, inc=1, device_id=(gg, tt), device_id_type=MESH)
    for gg in others:
        pl.semaphore_signal(barrier, inc=1, device_id=(gg, t), device_id_type=MESH)

    col = lax.broadcasted_iota(jnp.int32, (1, 128), 1) + t * 128
    live_row = jnp.concatenate([(col < sizes_ref[a]).astype(f32) for a in range(4)], axis=0)
    s_row = live_row * rs_ref[...]
    own_half = lax.rem(t, 2)
    goal_half = t // 2
    skel = skel_ref[0]
    sk_lo, sk_hi = skel[:, :128], skel[:, 128:]
    goals = jnp.where(goal_half == 0, sk_lo, sk_hi)
    sources = jnp.where(own_half == 0, sk_lo, sk_hi)
    skb[g] = jnp.concatenate([sources, jnp.zeros((1, 128), f32)], axis=0)
    for a in range(4):
        hal1[4 + t, a] = jnp.concatenate([pts_ref[c, a : a + 1, :] for c in range(3)] + [s_row[a : a + 1]], axis=0)
    stacked = jnp.concatenate(
        [s_row, live_row] + [pts_ref[c] for c in range(3)] + [goals, jnp.zeros((128 - 23, 128), f32)], axis=0
    )
    cols = stacked.T
    lane = lax.broadcasted_iota(jnp.int32, (128, 128), 1)

    def spread(i):
        return jnp.broadcast_to(cols[:, i : i + 1], (128, 128))

    part_lo = jnp.zeros((128, 128), f32)
    part_hi = jnp.zeros((128, 128), f32)
    for a in range(4):
        s_b = spread(a)
        fcol[a] = s_b
        live_col[a] = spread(4 + a)
        part_lo = part_lo + basis_ref[a, :, :128] * s_b
        part_hi = part_hi + basis_ref[a, :, 128:] * s_b
    abuf[0, t, 0:1] = jnp.sum(part_lo, axis=0, keepdims=True)
    abuf[0, t, 1:2] = jnp.sum(part_hi, axis=0, keepdims=True)
    for c in range(3):
        tfar[c] = spread(20 + c)
        for a in range(4):
            tnear[a * 3 + c] = spread(8 + c * 4 + a)

    pl.semaphore_wait(barrier, 127 + 9)

    def send(src, dst, which, dev):
        pltpu.make_async_remote_copy(
            src_ref=src, dst_ref=dst, send_sem=ssem.at[which], recv_sem=rsem.at[which], device_id=dev, device_id_type=MESH
        ).start()

    def wait(ref, which):
        pltpu.make_async_copy(ref, ref, rsem.at[which]).wait()

    def drain(ref, which):
        pltpu.make_async_copy(ref, ref, ssem.at[which]).wait()

    def to_tiles(buf, which):
        for tt in tiles:
            send(buf.at[t], buf.at[t], which, (g, tt))

    def to_others(buf, which):
        for gg in others:
            send(buf.at[g], buf.at[g], which, (gg, t))

    def to_halo(buf, which):
        for tt in tiles:
            send(buf.at[4 + t], buf.at[8 + t], which, (left, tt))
            send(buf.at[4 + t], buf.at[t], which, (right, tt))
            send(buf.at[4 + t], buf.at[4 + t], which, (g, tt))
        send(buf.at[4 + t], buf.at[8 + t], which, (left, t))
        send(buf.at[4 + t], buf.at[t], which, (right, t))

    def neighbour(a, slot):
        rel = jnp.clip(lax.rem(near_ref[a, slot] - 4 * g + (4 + 512), 512), 0, 11)
        return rel // 4, lax.rem(rel, 4)

    def near_values():
        def body(i, carry):
            a, slot, tt = i // 16, lax.rem(i // 4, 4), lax.rem(i, 4)
            gg, leaf = neighbour(a, slot)
            src = hal1[gg * 4 + tt, leaf]
            d0 = tnear[a * 3] - src[0:1]
            d1 = tnear[a * 3 + 1] - src[1:2]
            d2 = tnear[a * 3 + 2] - src[2:3]
            gnear[i] = lax.rsqrt(d0 * d0 + d1 * d1 + d2 * d2 + spread_sq)
            return carry

        lax.fori_loop(0, 64, body, 0)

    def near_apply(value):
        def leaf_body(a, carry):
            def body(j, acc):
                slot, tt = j // 4, lax.rem(j, 4)
                gg, leaf = neighbour(a, slot)
                weight = jnp.where(slot < count_ref[a], near_scale, 0.0)
                return acc + gnear[a * 16 + j] * (value(gg * 4 + tt, leaf) * weight)

            acc_near[a] = lax.fori_loop(0, 16, body, jnp.zeros((128, 128), f32), unroll=4)
            return carry

        lax.fori_loop(0, 4, leaf_body, 0)

    def far_values():
        def body(b, carry):
            src = skb[b]
            d0 = tfar[0] - src[0:1]
            d1 = tfar[1] - src[1:2]
            d2 = tfar[2] - src[2:3]
            gfar[b] = lax.rsqrt(d0 * d0 + d1 * d1 + d2 * d2 + spread_sq)
            return carry

        lax.fori_loop(0, 128, body, 0)

    def far_apply(n):
        def body(b, acc):
            weight = jnp.where(mask_ref[0, b] != 0, far_scale, 0.0)
            return acc + gfar[b] * (cbuf[n, b] * weight)

        acc = lax.fori_loop(0, 128, body, jnp.zeros((128, 128), f32), unroll=8)
        return jnp.sum(acc.T, axis=0, keepdims=True)

    def coef_sum(n):
        mine = abuf[n, 0] + abuf[n, 1] + abuf[n, 2] + abuf[n, 3]
        cbuf[n, g] = jnp.where(own_half == 0, mine[0:1], mine[1:2])

    def finish(n):
        sky_lo = pbuf[n, 0] + pbuf[n, 1]
        sky_hi = pbuf[n, 2] + pbuf[n, 3]
        rows = jnp.zeros((128, 128), f32)
        part_lo = jnp.zeros((128, 128), f32)
        part_hi = jnp.zeros((128, 128), f32)
        for a in range(4):
            b_lo, b_hi = basis_ref[a, :, :128], basis_ref[a, :, 128:]
            total = acc_near[a] + b_lo * sky_lo + b_hi * sky_hi
            image = live_col[a] * (fcol[a] + jnp.sum(total, axis=1, keepdims=True))
            rows = jnp.where(lane == a, image, rows)
            if n == 0:
                fcol[a] = image
                part_lo = part_lo + b_lo * image
                part_hi = part_hi + b_hi * image
        if n == 0:
            abuf[1, t, 0:1] = jnp.sum(part_lo, axis=0, keepdims=True)
            abuf[1, t, 1:2] = jnp.sum(part_hi, axis=0, keepdims=True)
        return rows.T[0:4]

    to_tiles(abuf.at[0], COEF_ONE)
    to_halo(hal1, HALO_ONE)
    to_others(skb, SKEL)
    wait(abuf.at[0, pl.ds(0, 3)], COEF_ONE)
    coef_sum(0)
    to_others(cbuf.at[0], FAR_ONE)
    wait(skb.at[pl.ds(0, 127)], SKEL)
    far_values()
    wait(cbuf.at[0, pl.ds(0, 127)], FAR_ONE)
    pbuf[0, t] = far_apply(0)
    to_tiles(pbuf.at[0], SKY_ONE)
    wait(hal1.at[pl.ds(0, 11)], HALO_ONE)
    near_values()
    near_apply(lambda slot, leaf: hal1[slot, leaf][3:4])
    wait(pbuf.at[0, pl.ds(0, 3)], SKY_ONE)
    a_row = finish(0)

    to_tiles(abuf.at[1], COEF_TWO)
    for a in range(4):
        hal2[4 + t, a] = a_row[a : a + 1]
    to_halo(hal2, HALO_TWO)
    wait(abuf.at[1, pl.ds(0, 3)], COEF_TWO)
    coef_sum(1)
    to_others(cbuf.at[1], FAR_TWO)
    wait(hal2.at[pl.ds(0, 11)], HALO_TWO)
    near_apply(lambda slot, leaf: hal2[slot, leaf])
    wait(cbuf.at[1, pl.ds(0, 127)], FAR_TWO)
    pbuf[1, t] = far_apply(1)
    to_tiles(pbuf.at[1], SKY_TWO)
    wait(pbuf.at[1, pl.ds(0, 3)], SKY_TWO)
    b_row = finish(1)

    pairs = [s_row * s_row, s_row * a_row, s_row * b_row, a_row * a_row, a_row * b_row, b_row * b_row]
    sums = jnp.concatenate([jnp.sum(p, axis=0, keepdims=True) for p in pairs] + [jnp.zeros((2, 128), f32)], axis=0)
    sums = jnp.sum(sums, axis=1, keepdims=True)
    picked = lax.broadcasted_iota(jnp.int32, (8, 128), 0) == lax.broadcasted_iota(jnp.int32, (8, 128), 1)
    rtile[t] = jnp.sum(jnp.where(picked, sums, 0.0), axis=0, keepdims=True)
    to_tiles(rtile, SUM_TILE)
    wait(rtile.at[pl.ds(0, 3)], SUM_TILE)
    rblk[g] = rtile[0] + rtile[1] + rtile[2] + rtile[3]
    to_others(rblk, SUM_BLK)
    wait(rblk.at[pl.ds(0, 127)], SUM_BLK)
    dots = jnp.sum(rblk[...], axis=0)
    ss, sa, sb, aa, ab, bb = [dots[:, i : i + 1] for i in range(6)]

    beta_sq = ss + norm_eps
    beta = jnp.sqrt(beta_sq)
    h11 = sa / beta_sq
    h21_sq = jnp.maximum((aa - 2.0 * h11 * sa + h11 * h11 * ss) / beta_sq, 0.0) + norm_eps
    h21 = jnp.sqrt(h21_sq)
    h12 = (sb - h11 * sa) / (beta_sq * h21)
    h22 = (ab - h11 * aa - h11 * sb + h11 * h11 * sa) / (beta_sq * h21_sq)
    w_sq = (bb - 2.0 * h11 * ab + h11 * h11 * aa) / (beta_sq * h21_sq)
    first_sq = ss / beta_sq
    second_sq = (h21_sq - norm_eps) / h21_sq
    cross = h11 * (1.0 - first_sq) / h21
    rest_sq = w_sq - h12 * h12 * (2.0 - first_sq) - h22 * h22 * (2.0 - second_sq) + 2.0 * h12 * h22 * cross
    h32_sq = jnp.maximum(rest_sq, 0.0) + norm_eps
    m_aa = h11 * h11 + h21_sq
    m_ab = h11 * h12 + h21 * h22
    m_bb = h12 * h12 + h22 * h22 + h32_sq
    determ = m_aa * m_bb - m_ab * m_ab
    y_one = beta * (m_bb * h11 - m_ab * h12) / determ
    y_two = beta * (m_aa * h12 - m_ab * h11) / determ
    c_one = y_one / beta
    c_two = y_two / (beta * h21)
    sol_ref[...] = c_one * s_row + c_two * (a_row - h11 * s_row)
    res_ref[...] = s_row - c_one * a_row - c_two * (b_row - h11 * a_row)

    drain(hal1.at[pl.ds(0, 11)], HALO_ONE)
    drain(hal2.at[pl.ds(0, 11)], HALO_TWO)
    drain(abuf.at[0, pl.ds(0, 3)], COEF_ONE)
    drain(abuf.at[1, pl.ds(0, 3)], COEF_TWO)
    drain(skb.at[pl.ds(0, 127)], SKEL)
    drain(cbuf.at[0, pl.ds(0, 127)], FAR_ONE)
    drain(cbuf.at[1, pl.ds(0, 127)], FAR_TWO)
    drain(pbuf.at[0, pl.ds(0, 3)], SKY_ONE)
    drain(pbuf.at[1, pl.ds(0, 3)], SKY_TWO)
    drain(rtile.at[pl.ds(0, 3)], SUM_TILE)
    drain(rblk.at[pl.ds(0, 127)], SUM_BLK)


def per_device(right_side, points, basis, skeleton, cluster_sizes, near_list, near_count, far_mask):
    vmem = pl.BlockSpec(memory_space=pltpu.VMEM)
    smem = pl.BlockSpec(memory_space=pltpu.SMEM)
    out = jax.ShapeDtypeStruct((4, 128), f32)
    return pl.pallas_call(
        kernel,
        out_shape=(out, out),
        in_specs=[vmem] * 4 + [smem] * 4,
        out_specs=(vmem, vmem),
        scratch_shapes=[
            pltpu.VMEM((12, 4, 4, 128), f32),
            pltpu.VMEM((12, 4, 1, 128), f32),
            pltpu.VMEM((2, 4, 2, 128), f32),
            pltpu.VMEM((128, 4, 128), f32),
            pltpu.VMEM((2, 128, 1, 128), f32),
            pltpu.VMEM((2, 4, 1, 128), f32),
            pltpu.VMEM((4, 1, 128), f32),
            pltpu.VMEM((128, 1, 128), f32),
            pltpu.VMEM((128, 128, 128), f32),
            pltpu.VMEM((64, 128, 128), f32),
            pltpu.VMEM((3, 128, 128), f32),
            pltpu.VMEM((12, 128, 128), f32),
            pltpu.VMEM((4, 128, 128), f32),
            pltpu.VMEM((4, 128, 128), f32),
            pltpu.VMEM((4, 128, 128), f32),
            pltpu.SemaphoreType.DMA((EXCHANGES,)),
            pltpu.SemaphoreType.DMA((EXCHANGES,)),
        ],
        compiler_params=pltpu.CompilerParams(collective_id=0, has_side_effects=True, vmem_limit_bytes=48 * 2**20),
    )(right_side, points, basis, skeleton, cluster_sizes, near_list, near_count, far_mask)


def solution(mesh):
    placed = (
        P("blk", "tile"),
        P(None, "blk", "tile"),
        P("blk", "tile", None),
        P("blk", None, None),
        P("blk"),
        P("blk", None),
        P("blk"),
        P("blk", None),
    )
    return jax.shard_map(
        per_device,
        mesh=mesh,
        in_specs=placed,
        out_specs=(P("blk", "tile"), P("blk", "tile")),
        check_vma=False,
    )
```

time: 1850 us -> 71.5 us (0.04)
  blocking collectives: 1110 us -> 0 us
  matrix products: 255 us -> 0 us
  local copies, waits for them, and re-layouts: 221 us -> 4.93 us
  loops' own time: 150 us -> 0 us
  other arithmetic: 67.1 us -> 0 us
  Pallas kernels: 0 us -> 65.6 us
  starting transfers between devices: 25.2 us -> 0 us
    psum x8 -> x0, blocking collectives: 591 us -> none  [the longest x1 102 us: per_device(): lax.psum(jnp.sum(start_vec * start_vec), ('blk', 'tile')) + norm_eps]
    all_gather x6 -> x0, blocking collectives: 497 us -> none  [the longest x2 307 us: far_field(): coef_piece = lax.all_gather(coef, 'blk', axis=0, tiled=True)]
    dot_general x292 -> x0, matrix products: 255 us -> none  [the longest x256 205 us: one_sub(): jnp.dot(coupling(target_sky, pts_piece[number]), coef_piece[number], prec...]
    dynamic_slice x353 -> x0, local copies, waits for them, and re-layouts: 212 us -> none  [the longest x256 153 us: one_sub(): weight = lax.dynamic_index_in_dim(far_row, number, 0, keepdims=False)]
    another operation x4 -> x0, loops' own time: 150 us -> none  [the longest x2 146 us: near_field(): lax.scan(slot_step, empty, jnp.arange(leaf_dev * slot_count))]
    pallas_call x0 -> x1, Pallas kernels: none -> 65.6 us  [per_device(): pl.pallas_call(kernel, out_shape=(out, out), in_specs=[vmem] * 4 + [smem]...]
    reduce_sum x294 -> x0, other arithmetic: 42.8 us -> none  [the longest x288 36.1 us: coupling(): dist_sq = jnp.sum((targets[:, :, None] - sources[:, None, :]) ** 2, axis=0)]
    ppermute x6 -> x0, starting transfers between devices: 25.2 us -> none  [the longest x3 12.8 us: extended(): lax.ppermute(lax.slice_in_dim(block, 0, width, axis=dim), axis, backward)]
  transfers between devices with their start and end apart: 6 -> 0, of which waited for: 0 -> 0; matrix products, arithmetic and copies ran while one was open for 21% -> 0% of each run, Pallas kernels for 0% -> 0%
where the time goes in v1:
time: 71.5 us; the launch traced here: 71.2 us
  Pallas kernels  65.6 us (92%)
  local copies, waits for them, and re-layouts  4.93 us (7%)
    pallas_call x1, Pallas kernels, per_device(): pl.pallas_call(kernel, out_shape=(out, out), in_specs=[vmem] * 4 + [smem]...  65.6 us
    unnamed x17, local copies, waits for them, and re-layouts  4.93 us

profile of v1, /device:TPU:1, one launch (start us, length us, event | category | flops | bytes accessed | tf_op | source)
XLA Modules:
  0.0 71.2 jit_solution(2280750349360493133)
XLA Ops:
  0.6 0.0 copy-start.5
  0.6 0.0 copy-start.4
  0.7 0.0 copy-start.1
  0.7 0.7 copy.10.skel_ref
  1.4 0.0 copy-done.5
  1.4 0.0 copy-done.4
  1.4 0.0 copy-done.1
  1.4 0.0 copy-start
  1.4 1.0 %copy-done = f32[4,128,256]{2,1,0:T(8,128)S(1)} copy-done((f32[4,128,256]{2,1,0:T(8,128)S(1)}, f32[4,128,256]{2,1,0:T(8,128)}, u32[]{:S(2)}) %copy-start) | copy-done | bytes 524312
  2.4 0.0 copy-start.2
  2.4 0.7 copy-done.2
  3.1 0.0 copy-start.3
  3.1 0.7 copy-done.3
  3.8 0.0 copy-start.6
  3.8 0.7 copy-done.6
  4.4 65.6 %shard_map.95 = (f32[4,128]{1,0:T(4,128)S(1)}, f32[4,128]{1,0:T(4,128)S(1)}) custom-call(f32[4,128]{1,0:T(4,128)S(1)} %copy-done.2, f32[3,4,128]{2,1,0:T(4,128)S(1)} %copy-done.1, f32[4,128,256]{2,1,0:T(8,128)S(1)} %copy-done, f32[1,3,256]{2,1,0:T(4,128)S(1)} %copy.10.skel_ref, s32[4]{0:T(128)S(1)} %copy-done.4, s32[4,4]{1,0:T(4,128)S(1)} %copy-done.3, ...), custom_call_target="tpu_custom_call" | custom-call | tf_op jit(solution)/shard_map/pallas_call | solution.py:281
  70.0 0.6 copy.13
  70.6 0.6 copy.14
Async XLA Ops:
  0.6 0.7 %copy-start.5 = (s32[4]{0:T(128)S(1)}, s32[4]{0:T(128)}, u32[]{:S(2)}) copy-start(s32[4]{0:T(128)} %count_ref.1) | copy-start | bytes 52
  0.6 0.7 %copy-start.4 = (s32[4]{0:T(128)S(1)}, s32[4]{0:T(128)}, u32[]{:S(2)}) copy-start(s32[4]{0:T(128)} %sizes_ref.1) | copy-start | bytes 52
  0.7 0.7 %copy-start.1 = (f32[3,4,128]{2,1,0:T(4,128)S(1)}, f32[3,4,128]{2,1,0:T(4,128)}, u32[]{:S(2)}) copy-start(f32[3,4,128]{2,1,0:T(4,128)} %pts_ref.1) | copy-start | bytes 18436
  1.4 1.0 %copy-start = (f32[4,128,256]{2,1,0:T(8,128)S(1)}, f32[4,128,256]{2,1,0:T(8,128)}, u32[]{:S(2)}) copy-start(f32[4,128,256]{2,1,0:T(8,128)} %basis_ref.1) | copy-start | bytes 1572868
  2.4 0.7 copy-start.2
  3.1 0.7 copy-start.3
  3.8 0.7 copy-start.6

commit v2 on v1

--- a/solution.py
+++ b/solution.py
@@ -29,16 +29,27 @@
 
 
 def kernel(
+    rs_hbm, pts_hbm, basis_hbm, skel_hbm, sizes_hbm, near_hbm, count_hbm, mask_hbm,
+    out_ref,
     rs_ref, pts_ref, basis_ref, skel_ref, sizes_ref, near_ref, count_ref, mask_ref,
-    sol_ref, res_ref,
     hal1, hal2, abuf, skb, cbuf, pbuf, rtile, rblk,
     gfar, gnear, tfar, tnear, fcol, live_col, acc_near,
-    ssem, rsem,
+    ssem, rsem, lsem,
 ):
     g = lax.axis_index("blk")
     t = lax.axis_index("tile")
     near_scale = 2.0 / math.sqrt(512 * 4)
     far_scale = 4.0 / math.sqrt(256 * 128)
+
+    loads = [
+        pltpu.make_async_copy(src, dst, lsem.at[i])
+        for i, (src, dst) in enumerate(
+            [(sizes_hbm, sizes_ref), (rs_hbm, rs_ref), (basis_hbm, basis_ref), (pts_hbm, pts_ref), (skel_hbm, skel_ref),
+             (near_hbm, near_ref), (count_hbm, count_ref), (mask_hbm, mask_ref)]
+        )
+    ]
+    for load in loads:
+        load.start()
 
     core, z, x, yl = lax.rem(g, 2), lax.rem(g // 2, 8), lax.rem(g // 16, 4), g // 64
     low = {(dz, dc): lax.rem(z + dz, 8) * 2 + lax.rem(core + dc, 2) for dz in range(8) for dc in range(2)}
@@ -54,41 +65,41 @@
     for gg in others:
         pl.semaphore_signal(barrier, inc=1, device_id=(gg, t), device_id_type=MESH)
 
+    loads[0].wait()
+    loads[1].wait()
     col = lax.broadcasted_iota(jnp.int32, (1, 128), 1) + t * 128
     live_row = jnp.concatenate([(col < sizes_ref[a]).astype(f32) for a in range(4)], axis=0)
     s_row = live_row * rs_ref[...]
     own_half = lax.rem(t, 2)
     goal_half = t // 2
-    skel = skel_ref[0]
-    sk_lo, sk_hi = skel[:, :128], skel[:, 128:]
-    goals = jnp.where(goal_half == 0, sk_lo, sk_hi)
-    sources = jnp.where(own_half == 0, sk_lo, sk_hi)
-    skb[g] = jnp.concatenate([sources, jnp.zeros((1, 128), f32)], axis=0)
-    for a in range(4):
-        hal1[4 + t, a] = jnp.concatenate([pts_ref[c, a : a + 1, :] for c in range(3)] + [s_row[a : a + 1]], axis=0)
-    stacked = jnp.concatenate(
-        [s_row, live_row] + [pts_ref[c] for c in range(3)] + [goals, jnp.zeros((128 - 23, 128), f32)], axis=0
-    )
-    cols = stacked.T
     lane = lax.broadcasted_iota(jnp.int32, (128, 128), 1)
 
-    def spread(i):
+    def columns(rows):
+        return jnp.concatenate(rows + [jnp.zeros((128 - sum(r.shape[0] for r in rows), 128), f32)], axis=0).T
+
+    def spread(cols, i):
         return jnp.broadcast_to(cols[:, i : i + 1], (128, 128))
 
+    cols = columns([s_row, live_row])
+    loads[2].wait()
     part_lo = jnp.zeros((128, 128), f32)
     part_hi = jnp.zeros((128, 128), f32)
     for a in range(4):
-        s_b = spread(a)
+        s_b = spread(cols, a)
         fcol[a] = s_b
-        live_col[a] = spread(4 + a)
+        live_col[a] = spread(cols, 4 + a)
         part_lo = part_lo + basis_ref[a, :, :128] * s_b
         part_hi = part_hi + basis_ref[a, :, 128:] * s_b
     abuf[0, t, 0:1] = jnp.sum(part_lo, axis=0, keepdims=True)
     abuf[0, t, 1:2] = jnp.sum(part_hi, axis=0, keepdims=True)
-    for c in range(3):
-        tfar[c] = spread(20 + c)
-        for a in range(4):
-            tnear[a * 3 + c] = spread(8 + c * 4 + a)
+    for load in loads[3:]:
+        load.wait()
+    for a in range(4):
+        hal1[4 + t, a] = jnp.concatenate([pts_ref[c, a : a + 1, :] for c in range(3)] + [s_row[a : a + 1]], axis=0)
+    sk_lo = jnp.concatenate([skel_ref[c, :, :128] for c in range(3)], axis=0)
+    sk_hi = jnp.concatenate([skel_ref[c, :, 128:] for c in range(3)], axis=0)
+    goals = jnp.where(goal_half == 0, sk_lo, sk_hi)
+    skb[g, 0:3] = jnp.where(own_half == 0, sk_lo, sk_hi)
 
     pl.semaphore_wait(barrier, 127 + 9)
 
@@ -194,11 +205,17 @@
 
     to_tiles(abuf.at[0], COEF_ONE)
     to_halo(hal1, HALO_ONE)
-    to_others(skb, SKEL)
+    for gg in others:
+        send(skb.at[g, pl.ds(0, 3)], skb.at[g, pl.ds(0, 3)], SKEL, (gg, t))
+    cols = columns([pts_ref[c] for c in range(3)] + [goals])
+    for c in range(3):
+        tfar[c] = spread(cols, 12 + c)
+        for a in range(4):
+            tnear[a * 3 + c] = spread(cols, c * 4 + a)
     wait(abuf.at[0, pl.ds(0, 3)], COEF_ONE)
     coef_sum(0)
     to_others(cbuf.at[0], FAR_ONE)
-    wait(skb.at[pl.ds(0, 127)], SKEL)
+    wait(skb.at[pl.ds(0, 127), pl.ds(0, 3)], SKEL)
     far_values()
     wait(cbuf.at[0, pl.ds(0, 127)], FAR_ONE)
     pbuf[0, t] = far_apply(0)
@@ -258,14 +275,14 @@
     y_two = beta * (m_aa * h12 - m_ab * h11) / determ
     c_one = y_one / beta
     c_two = y_two / (beta * h21)
-    sol_ref[...] = c_one * s_row + c_two * (a_row - h11 * s_row)
-    res_ref[...] = s_row - c_one * a_row - c_two * (b_row - h11 * a_row)
+    out_ref[0:4] = c_one * s_row + c_two * (a_row - h11 * s_row)
+    out_ref[4:8] = s_row - c_one * a_row - c_two * (b_row - h11 * a_row)
 
     drain(hal1.at[pl.ds(0, 11)], HALO_ONE)
     drain(hal2.at[pl.ds(0, 11)], HALO_TWO)
     drain(abuf.at[0, pl.ds(0, 3)], COEF_ONE)
     drain(abuf.at[1, pl.ds(0, 3)], COEF_TWO)
-    drain(skb.at[pl.ds(0, 127)], SKEL)
+    drain(skb.at[pl.ds(0, 127), pl.ds(0, 3)], SKEL)
     drain(cbuf.at[0, pl.ds(0, 127)], FAR_ONE)
     drain(cbuf.at[1, pl.ds(0, 127)], FAR_TWO)
     drain(pbuf.at[0, pl.ds(0, 3)], SKY_ONE)
@@ -276,14 +293,21 @@
 
 def per_device(right_side, points, basis, skeleton, cluster_sizes, near_list, near_count, far_mask):
     vmem = pl.BlockSpec(memory_space=pltpu.VMEM)
-    smem = pl.BlockSpec(memory_space=pltpu.SMEM)
-    out = jax.ShapeDtypeStruct((4, 128), f32)
-    return pl.pallas_call(
+    hbm = pl.BlockSpec(memory_space=pltpu.HBM)
+    both = pl.pallas_call(
         kernel,
-        out_shape=(out, out),
-        in_specs=[vmem] * 4 + [smem] * 4,
-        out_specs=(vmem, vmem),
+        out_shape=jax.ShapeDtypeStruct((8, 128), f32),
+        in_specs=[hbm] * 8,
+        out_specs=vmem,
         scratch_shapes=[
+            pltpu.VMEM((4, 128), f32),
+            pltpu.VMEM((3, 4, 128), f32),
+            pltpu.VMEM((4, 128, 256), f32),
+            pltpu.VMEM((3, 1, 256), f32),
+            pltpu.SMEM((4,), jnp.int32),
+            pltpu.SMEM((4, 4), jnp.int32),
+            pltpu.SMEM((4,), jnp.int32),
+            pltpu.SMEM((1, 128), jnp.int32),
             pltpu.VMEM((12, 4, 4, 128), f32),
             pltpu.VMEM((12, 4, 1, 128), f32),
             pltpu.VMEM((2, 4, 2, 128), f32),
@@ -301,9 +325,11 @@
             pltpu.VMEM((4, 128, 128), f32),
             pltpu.SemaphoreType.DMA((EXCHANGES,)),
             pltpu.SemaphoreType.DMA((EXCHANGES,)),
+            pltpu.SemaphoreType.DMA((8,)),
         ],
-        compiler_params=pltpu.CompilerParams(collective_id=0, has_side_effects=True, vmem_limit_bytes=48 * 2**20),
-    )(right_side, points, basis, skeleton, cluster_sizes, near_list, near_count, far_mask)
+        compiler_params=pltpu.CompilerParams(collective_id=0, has_side_effects=True, vmem_limit_bytes=64 * 2**20),
+    )(right_side, points, basis, skeleton.transpose(1, 0, 2), cluster_sizes, near_list, near_count, far_mask)
+    return both[0:4], both[4:8]
 
 
 def solution(mesh):

time: 71.5 us -> 66.4 us (0.929)
  local copies, waits for them, and re-layouts: 4.93 us -> 1.33 us
  Pallas kernels: 65.6 us -> 64.3 us
    unnamed x17 -> x0, local copies, waits for them, and re-layouts: 4.93 us -> none
    slice x0 -> x1, local copies, waits for them, and re-layouts: none -> 1.33 us  [per_device(): return (both[0:4], both[4:8])]
    pallas_call x1, Pallas kernels: 65.6 us -> 64.3 us  [per_device(): pl.pallas_call(kernel, out_shape=jax.ShapeDtypeStruct((8, 128), f32), in_...]
where the time goes in v2:
time: 66.4 us; the launch traced here: 66.3 us
  Pallas kernels  64.3 us (97%)
  local copies, waits for them, and re-layouts  1.33 us (2%)
    pallas_call x1, Pallas kernels, per_device(): pl.pallas_call(kernel, out_shape=jax.ShapeDtypeStruct((8, 128), f32), in_...  64.3 us
    slice x1, local copies, waits for them, and re-layouts, per_device(): return (both[0:4], both[4:8])  1.33 us

profile of v2, /device:TPU:1, one launch (start us, length us, event | category | flops | bytes accessed | tf_op | source)
XLA Modules:
  0.0 66.3 jit_solution(193842556877447459)
XLA Ops:
  0.6 64.3 %shard_map.95 = f32[8,128]{1,0:T(8,128)} custom-call(f32[4,128]{1,0:T(4,128)} %rs_hbm.1, f32[3,4,128]{2,1,0:T(4,128)} %pts_hbm.1, f32[4,128,256]{2,1,0:T(8,128)} %basis_hbm.1, f32[3,1,256]{2,1,0:T(1,128)} %bitcast.1, s32[4]{0:T(128)} %sizes_hbm.1, s32[4,4]{1,0:T(4,128)} %near_hbm.1, s32[4]{0:T(128)} %count_hbm.1, s32[1,128]{1,0:T(1,128)} %mask_hbm.1), custom_call_target="tpu_custom_call" | custom-call | tf_op jit(solution)/shard_map/pallas_call | solution.py:297
  65.0 1.3 %fusion = (f32[4,128]{1,0:T(4,128)}, f32[4,128]{1,0:T(4,128)}) fusion(f32[8,128]{1,0:T(8,128)} %shard_map.95), kind=kLoop, calls=%fused_computation | loop fusion | bytes 8192 | tf_op jit(solution)/shard_map/slice | solution.py:332

commit v3 on v2

--- a/solution.py
+++ b/solution.py
@@ -13,7 +13,7 @@
 spread_sq = 0.25
 norm_eps = 1e-06
 
-HALO_ONE, HALO_TWO, COEF_ONE, COEF_TWO, SKEL, FAR_ONE, FAR_TWO, SKY_ONE, SKY_TWO, SUM_TILE, SUM_BLK = range(11)
+HALO_ONE, HALO_TWO, COEF, SKEL, FAR_ONE, FAR_TWO, SKY_ONE, SKY_TWO, MIX_PART, MIX_ALL, SUMS = range(11)
 EXCHANGES = 11
 
 
@@ -32,8 +32,8 @@
     rs_hbm, pts_hbm, basis_hbm, skel_hbm, sizes_hbm, near_hbm, count_hbm, mask_hbm,
     out_ref,
     rs_ref, pts_ref, basis_ref, skel_ref, sizes_ref, near_ref, count_ref, mask_ref,
-    hal1, hal2, abuf, skb, cbuf, pbuf, rtile, rblk,
-    gfar, gnear, tfar, tnear, fcol, live_col, acc_near,
+    hal1, hal2, abuf, skb, cbuf, pbuf, rblk, mix_own, mix_part, mix_all, mix,
+    gfar, gnear, tfar, tnear, scol, ucol, acol, live_col,
     ssem, rsem, lsem,
 ):
     g = lax.axis_index("blk")
@@ -84,14 +84,18 @@
     loads[2].wait()
     part_lo = jnp.zeros((128, 128), f32)
     part_hi = jnp.zeros((128, 128), f32)
+    s_sq = jnp.zeros((128, 128), f32)
     for a in range(4):
         s_b = spread(cols, a)
-        fcol[a] = s_b
+        scol[a] = s_b
+        s_sq = s_sq + s_b * s_b
         live_col[a] = spread(cols, 4 + a)
         part_lo = part_lo + basis_ref[a, :, :128] * s_b
         part_hi = part_hi + basis_ref[a, :, 128:] * s_b
-    abuf[0, t, 0:1] = jnp.sum(part_lo, axis=0, keepdims=True)
-    abuf[0, t, 1:2] = jnp.sum(part_hi, axis=0, keepdims=True)
+    abuf[t, 0:1] = jnp.sum(part_lo, axis=0, keepdims=True)
+    abuf[t, 1:2] = jnp.sum(part_hi, axis=0, keepdims=True)
+    abuf[t, 2:3] = jnp.sum(s_sq, axis=0, keepdims=True)
+    abuf[t, 3:4] = jnp.zeros((1, 128), f32)
     for load in loads[3:]:
         load.wait()
     for a in range(4):
@@ -134,42 +138,42 @@
         rel = jnp.clip(lax.rem(near_ref[a, slot] - 4 * g + (4 + 512), 512), 0, 11)
         return rel // 4, lax.rem(rel, 4)
 
-    def near_values():
-        def body(i, carry):
-            a, slot, tt = i // 16, lax.rem(i // 4, 4), lax.rem(i, 4)
-            gg, leaf = neighbour(a, slot)
-            src = hal1[gg * 4 + tt, leaf]
-            d0 = tnear[a * 3] - src[0:1]
-            d1 = tnear[a * 3 + 1] - src[1:2]
-            d2 = tnear[a * 3 + 2] - src[2:3]
-            gnear[i] = lax.rsqrt(d0 * d0 + d1 * d1 + d2 * d2 + spread_sq)
-            return carry
-
-        lax.fori_loop(0, 64, body, 0)
-
-    def near_apply(value):
-        def leaf_body(a, carry):
-            def body(j, acc):
-                slot, tt = j // 4, lax.rem(j, 4)
+    def kernel_values(base, first, src):
+        x, y, z = src[0:1], src[1:2], src[2:3]
+        size = x * x + y * y + z * z + spread_sq
+        return lax.rsqrt((base[first] + size) + (base[first + 1] * x + base[first + 2] * y + base[first + 3] * z))
+
+    def near_apply(field, visit):
+        for a in range(4):
+            def body(slot, acc, a=a):
                 gg, leaf = neighbour(a, slot)
                 weight = jnp.where(slot < count_ref[a], near_scale, 0.0)
-                return acc + gnear[a * 16 + j] * (value(gg * 4 + tt, leaf) * weight)
-
-            acc_near[a] = lax.fori_loop(0, 16, body, jnp.zeros((128, 128), f32), unroll=4)
-            return carry
-
-        lax.fori_loop(0, 4, leaf_body, 0)
+                for tt in range(4):
+                    values, source = visit(a, slot, tt, gg * 4 + tt, leaf)
+                    acc = acc + values * (source * weight)
+                return acc
+
+            acc = lax.fori_loop(0, 4, body, jnp.zeros((128, 128), f32), unroll=2)
+            ucol[a] = live_col[a] * (field[a] + jnp.sum(acc, axis=1, keepdims=True))
+
+    def near_first():
+        def visit(a, slot, tt, place, leaf):
+            src = hal1[place, leaf]
+            values = kernel_values(tnear, a * 4, src)
+            gnear[a * 16 + slot * 4 + tt] = values
+            return values, src[3:4]
+
+        near_apply(scol, visit)
+
+    def near_second():
+        near_apply(acol, lambda a, slot, tt, place, leaf: (gnear[a * 16 + slot * 4 + tt], hal2[place, leaf]))
 
     def far_values():
         def body(b, carry):
-            src = skb[b]
-            d0 = tfar[0] - src[0:1]
-            d1 = tfar[1] - src[1:2]
-            d2 = tfar[2] - src[2:3]
-            gfar[b] = lax.rsqrt(d0 * d0 + d1 * d1 + d2 * d2 + spread_sq)
+            gfar[b] = kernel_values(tfar, 0, skb[b])
             return carry
 
-        lax.fori_loop(0, 128, body, 0)
+        lax.fori_loop(0, 128, body, 0, unroll=4)
 
     def far_apply(n):
         def body(b, acc):
@@ -179,78 +183,138 @@
         acc = lax.fori_loop(0, 128, body, jnp.zeros((128, 128), f32), unroll=8)
         return jnp.sum(acc.T, axis=0, keepdims=True)
 
-    def coef_sum(n):
-        mine = abuf[n, 0] + abuf[n, 1] + abuf[n, 2] + abuf[n, 3]
-        cbuf[n, g] = jnp.where(own_half == 0, mine[0:1], mine[1:2])
-
-    def finish(n):
-        sky_lo = pbuf[n, 0] + pbuf[n, 1]
-        sky_hi = pbuf[n, 2] + pbuf[n, 3]
+    def near_parts(n, fields):
+        lo = jnp.zeros((128, 128), f32)
+        hi = jnp.zeros((128, 128), f32)
+        prods = [jnp.zeros((128, 128), f32) for _ in range(len(fields) + 1)]
+        for a in range(4):
+            u = ucol[a]
+            lo = lo + basis_ref[a, :, :128] * u
+            hi = hi + basis_ref[a, :, 128:] * u
+            for i, field in enumerate(fields + [ucol]):
+                prods[i] = prods[i] + field[a] * u
+        pbuf[n, t, 1:2] = jnp.sum(lo, axis=0, keepdims=True)
+        pbuf[n, t, 2:3] = jnp.sum(hi, axis=0, keepdims=True)
+        packed = jnp.zeros((1, 128), f32)
+        for i, prod in enumerate(prods):
+            packed = jnp.where(lane[0:1] == i, jnp.sum(prod, axis=0, keepdims=True), packed)
+        pbuf[n, t, 3:4] = packed
+
+    def gathered(n):
+        low, high = pbuf[n, 0] + pbuf[n, 1], pbuf[n, 2] + pbuf[n, 3]
+        both = low + high
+        return low[0:1], high[0:1], both[1:2], both[2:3], both[3:4]
+
+    def mixed(sky_lo, sky_hi):
+        pair = columns([sky_lo, sky_hi])
+        col_lo, col_hi = spread(pair, 0), spread(pair, 1)
+        lo = mix[0] * col_lo + mix[1] * col_hi
+        hi = mix[2] * col_lo + mix[3] * col_hi
+        return jnp.sum(lo, axis=0, keepdims=True), jnp.sum(hi, axis=0, keepdims=True)
+
+    def image(sky_lo, sky_hi, keep):
         rows = jnp.zeros((128, 128), f32)
-        part_lo = jnp.zeros((128, 128), f32)
-        part_hi = jnp.zeros((128, 128), f32)
         for a in range(4):
-            b_lo, b_hi = basis_ref[a, :, :128], basis_ref[a, :, 128:]
-            total = acc_near[a] + b_lo * sky_lo + b_hi * sky_hi
-            image = live_col[a] * (fcol[a] + jnp.sum(total, axis=1, keepdims=True))
-            rows = jnp.where(lane == a, image, rows)
-            if n == 0:
-                fcol[a] = image
-                part_lo = part_lo + b_lo * image
-                part_hi = part_hi + b_hi * image
-        if n == 0:
-            abuf[1, t, 0:1] = jnp.sum(part_lo, axis=0, keepdims=True)
-            abuf[1, t, 1:2] = jnp.sum(part_hi, axis=0, keepdims=True)
+            far = basis_ref[a, :, :128] * sky_lo + basis_ref[a, :, 128:] * sky_hi
+            value = ucol[a] + live_col[a] * jnp.sum(far, axis=1, keepdims=True)
+            rows = jnp.where(lane == a, value, rows)
+            if keep:
+                acol[a] = value
         return rows.T[0:4]
 
-    to_tiles(abuf.at[0], COEF_ONE)
+    to_tiles(abuf, COEF)
     to_halo(hal1, HALO_ONE)
+
+    points_of = basis_ref[...].reshape(512, 256)
+    masked = points_of * live_col[...].reshape(512, 128)[:, 0:1]
+
+    def product(left, right):
+        return lax.dot_general(
+            left, right, (((0,), (0,)), ((), ())), precision=lax.Precision.HIGHEST, preferred_element_type=f32
+        )
+
+    upper = product(masked[:, :128], points_of)
+    lower = product(masked[:, 128:], points_of[:, 128:])
+    mix_own[0] = upper[0:96, :128]
+    mix_own[1, 0:32] = upper[96:128, :128]
+    mix_own[1, 32:96] = upper[0:64, 128:]
+    mix_own[2, 0:64] = upper[64:128, 128:]
+    mix_own[2, 64:96] = lower[0:32]
+    mix_own[3] = lower[32:128]
+    for tt in tiles:
+        send(mix_own.at[tt], mix_part.at[t], MIX_PART, (g, tt))
+    mix_part[t] = mix_own[t]
     for gg in others:
         send(skb.at[g, pl.ds(0, 3)], skb.at[g, pl.ds(0, 3)], SKEL, (gg, t))
-    cols = columns([pts_ref[c] for c in range(3)] + [goals])
-    for c in range(3):
-        tfar[c] = spread(cols, 12 + c)
+    goal_rows = [goals[c : c + 1] for c in range(3)]
+    cols = columns(
+        [-2.0 * pts_ref[c] for c in range(3)] + [sum(pts_ref[c] * pts_ref[c] for c in range(3))]
+        + [-2.0 * row for row in goal_rows] + [sum(row * row for row in goal_rows)]
+    )
+    for c in range(4):
+        tfar[(c + 1) % 4] = spread(cols, 16 + c)
         for a in range(4):
-            tnear[a * 3 + c] = spread(cols, c * 4 + a)
-    wait(abuf.at[0, pl.ds(0, 3)], COEF_ONE)
-    coef_sum(0)
+            tnear[a * 4 + (c + 1) % 4] = spread(cols, c * 4 + a)
+
+    wait(abuf.at[pl.ds(0, 3)], COEF)
+    parts = abuf[0] + abuf[1] + abuf[2] + abuf[3]
+    one_lo, one_hi, ss = parts[0:1], parts[1:2], parts[2:3]
+    cbuf[0, g] = jnp.where(own_half == 0, one_lo, one_hi)
     to_others(cbuf.at[0], FAR_ONE)
+    wait(hal1.at[pl.ds(0, 11)], HALO_ONE)
+    near_first()
+    wait(mix_part.at[pl.ds(0, 3)], MIX_PART)
+    mix_all[t] = mix_part[0] + mix_part[1] + mix_part[2] + mix_part[3]
+    to_tiles(mix_all, MIX_ALL)
+    near_parts(0, [scol])
     wait(skb.at[pl.ds(0, 127), pl.ds(0, 3)], SKEL)
     far_values()
     wait(cbuf.at[0, pl.ds(0, 127)], FAR_ONE)
-    pbuf[0, t] = far_apply(0)
+    pbuf[0, t, 0:1] = far_apply(0)
     to_tiles(pbuf.at[0], SKY_ONE)
-    wait(hal1.at[pl.ds(0, 11)], HALO_ONE)
-    near_values()
-    near_apply(lambda slot, leaf: hal1[slot, leaf][3:4])
+    wait(mix_all.at[pl.ds(0, 3)], MIX_ALL)
+    cross = jnp.concatenate([mix_all[1, 32:96], mix_all[2, 0:64]], axis=0)
+    mix[0] = jnp.concatenate([mix_all[0], mix_all[1, 0:32]], axis=0)
+    mix[1] = cross.T
+    mix[2] = cross
+    mix[3] = jnp.concatenate([mix_all[2, 64:96], mix_all[3]], axis=0)
     wait(pbuf.at[0, pl.ds(0, 3)], SKY_ONE)
-    a_row = finish(0)
-
-    to_tiles(abuf.at[1], COEF_TWO)
+    sky1_lo, sky1_hi, r1_lo, r1_hi, dots1 = gathered(0)
+    a_row = image(sky1_lo, sky1_hi, True)
+
     for a in range(4):
         hal2[4 + t, a] = a_row[a : a + 1]
     to_halo(hal2, HALO_TWO)
-    wait(abuf.at[1, pl.ds(0, 3)], COEF_TWO)
-    coef_sum(1)
+    m1_lo, m1_hi = mixed(sky1_lo, sky1_hi)
+    two_lo, two_hi = r1_lo + m1_lo, r1_hi + m1_hi
+    cbuf[1, g] = jnp.where(own_half == 0, two_lo, two_hi)
     to_others(cbuf.at[1], FAR_TWO)
     wait(hal2.at[pl.ds(0, 11)], HALO_TWO)
-    near_apply(lambda slot, leaf: hal2[slot, leaf])
+    near_second()
+    near_parts(1, [scol, acol])
     wait(cbuf.at[1, pl.ds(0, 127)], FAR_TWO)
-    pbuf[1, t] = far_apply(1)
+    pbuf[1, t, 0:1] = far_apply(1)
     to_tiles(pbuf.at[1], SKY_TWO)
     wait(pbuf.at[1, pl.ds(0, 3)], SKY_TWO)
-    b_row = finish(1)
-
-    pairs = [s_row * s_row, s_row * a_row, s_row * b_row, a_row * a_row, a_row * b_row, b_row * b_row]
-    sums = jnp.concatenate([jnp.sum(p, axis=0, keepdims=True) for p in pairs] + [jnp.zeros((2, 128), f32)], axis=0)
-    sums = jnp.sum(sums, axis=1, keepdims=True)
-    picked = lax.broadcasted_iota(jnp.int32, (8, 128), 0) == lax.broadcasted_iota(jnp.int32, (8, 128), 1)
-    rtile[t] = jnp.sum(jnp.where(picked, sums, 0.0), axis=0, keepdims=True)
-    to_tiles(rtile, SUM_TILE)
-    wait(rtile.at[pl.ds(0, 3)], SUM_TILE)
-    rblk[g] = rtile[0] + rtile[1] + rtile[2] + rtile[3]
-    to_others(rblk, SUM_BLK)
-    wait(rblk.at[pl.ds(0, 127)], SUM_BLK)
+    sky2_lo, sky2_hi, r2_lo, r2_hi, dots2 = gathered(1)
+
+    m2_lo, m2_hi = mixed(sky2_lo, sky2_hi)
+    rows = [
+        one_lo * sky1_lo + one_hi * sky1_hi,
+        one_lo * sky2_lo + one_hi * sky2_hi,
+        (r1_lo + two_lo) * sky1_lo + (r1_hi + two_hi) * sky1_hi,
+        two_lo * sky2_lo + two_hi * sky2_hi,
+        (2.0 * r2_lo + m2_lo) * sky2_lo + (2.0 * r2_hi + m2_hi) * sky2_hi,
+    ]
+    near_part = [dots1[:, 0:1], dots2[:, 0:1], dots1[:, 1:2], dots2[:, 1:2], dots2[:, 2:3]]
+    far_part = jnp.sum(jnp.concatenate(rows + [jnp.zeros((3, 128), f32)], axis=0), axis=1, keepdims=True)
+    packed = ss
+    for i in range(5):
+        packed = jnp.where(lane[0:1] == i + 1, near_part[i] + far_part[i : i + 1], packed)
+    rblk[g] = packed
+    to_others(rblk, SUMS)
+    b_row = image(sky2_lo, sky2_hi, False)
+    wait(rblk.at[pl.ds(0, 127)], SUMS)
     dots = jnp.sum(rblk[...], axis=0)
     ss, sa, sb, aa, ab, bb = [dots[:, i : i + 1] for i in range(6)]
 
@@ -264,8 +328,8 @@
     w_sq = (bb - 2.0 * h11 * ab + h11 * h11 * aa) / (beta_sq * h21_sq)
     first_sq = ss / beta_sq
     second_sq = (h21_sq - norm_eps) / h21_sq
-    cross = h11 * (1.0 - first_sq) / h21
-    rest_sq = w_sq - h12 * h12 * (2.0 - first_sq) - h22 * h22 * (2.0 - second_sq) + 2.0 * h12 * h22 * cross
+    cross_sq = h11 * (1.0 - first_sq) / h21
+    rest_sq = w_sq - h12 * h12 * (2.0 - first_sq) - h22 * h22 * (2.0 - second_sq) + 2.0 * h12 * h22 * cross_sq
     h32_sq = jnp.maximum(rest_sq, 0.0) + norm_eps
     m_aa = h11 * h11 + h21_sq
     m_ab = h11 * h12 + h21 * h22
@@ -280,15 +344,15 @@
 
     drain(hal1.at[pl.ds(0, 11)], HALO_ONE)
     drain(hal2.at[pl.ds(0, 11)], HALO_TWO)
-    drain(abuf.at[0, pl.ds(0, 3)], COEF_ONE)
-    drain(abuf.at[1, pl.ds(0, 3)], COEF_TWO)
+    drain(abuf.at[pl.ds(0, 3)], COEF)
+    drain(mix_part.at[pl.ds(0, 3)], MIX_PART)
+    drain(mix_all.at[pl.ds(0, 3)], MIX_ALL)
     drain(skb.at[pl.ds(0, 127), pl.ds(0, 3)], SKEL)
     drain(cbuf.at[0, pl.ds(0, 127)], FAR_ONE)
     drain(cbuf.at[1, pl.ds(0, 127)], FAR_TWO)
     drain(pbuf.at[0, pl.ds(0, 3)], SKY_ONE)
     drain(pbuf.at[1, pl.ds(0, 3)], SKY_TWO)
-    drain(rtile.at[pl.ds(0, 3)], SUM_TILE)
-    drain(rblk.at[pl.ds(0, 127)], SUM_BLK)
+    drain(rblk.at[pl.ds(0, 127)], SUMS)
 
 
 def per_device(right_side, points, basis, skeleton, cluster_sizes, near_list, near_count, far_mask):
@@ -310,16 +374,20 @@
             pltpu.SMEM((1, 128), jnp.int32),
             pltpu.VMEM((12, 4, 4, 128), f32),
             pltpu.VMEM((12, 4, 1, 128), f32),
-            pltpu.VMEM((2, 4, 2, 128), f32),
+            pltpu.VMEM((4, 4, 128), f32),
             pltpu.VMEM((128, 4, 128), f32),
             pltpu.VMEM((2, 128, 1, 128), f32),
-            pltpu.VMEM((2, 4, 1, 128), f32),
-            pltpu.VMEM((4, 1, 128), f32),
+            pltpu.VMEM((2, 4, 4, 128), f32),
             pltpu.VMEM((128, 1, 128), f32),
+            pltpu.VMEM((4, 96, 128), f32),
+            pltpu.VMEM((4, 96, 128), f32),
+            pltpu.VMEM((4, 96, 128), f32),
+            pltpu.VMEM((4, 128, 128), f32),
             pltpu.VMEM((128, 128, 128), f32),
             pltpu.VMEM((64, 128, 128), f32),
-            pltpu.VMEM((3, 128, 128), f32),
-            pltpu.VMEM((12, 128, 128), f32),
+            pltpu.VMEM((4, 128, 128), f32),
+            pltpu.VMEM((16, 128, 128), f32),
+            pltpu.VMEM((4, 128, 128), f32),
             pltpu.VMEM((4, 128, 128), f32),
             pltpu.VMEM((4, 128, 128), f32),
             pltpu.VMEM((4, 128, 128), f32),

time: 66.4 us -> 59.2 us (0.89)
  Pallas kernels: 64.3 us -> 57.1 us
    pallas_call x1, Pallas kernels: 64.3 us -> 57.1 us  [per_device(): pl.pallas_call(kernel, out_shape=jax.ShapeDtypeStruct((8, 128), f32), in_...]
where the time goes in v3:
time: 59.2 us; the launch traced here: 59.1 us
  Pallas kernels  57.1 us (96%)
  local copies, waits for them, and re-layouts  1.33 us (2%)
  between operations  0.64 us (1%)
    pallas_call x1, Pallas kernels, per_device(): pl.pallas_call(kernel, out_shape=jax.ShapeDtypeStruct((8, 128), f32), in_...  57.1 us
    slice x1, local copies, waits for them, and re-layouts, per_device(): return (both[0:4], both[4:8])  1.33 us

profile of v3, /device:TPU:1, one launch (start us, length us, event | category | flops | bytes accessed | tf_op | source)
XLA Modules:
  0.0 59.1 jit_solution(18113269284626795762)
XLA Ops:
  0.6 57.1 %shard_map.95 = f32[8,128]{1,0:T(8,128)} custom-call(f32[4,128]{1,0:T(4,128)} %rs_hbm.1, f32[3,4,128]{2,1,0:T(4,128)} %pts_hbm.1, f32[4,128,256]{2,1,0:T(8,128)} %basis_hbm.1, f32[3,1,256]{2,1,0:T(1,128)} %bitcast.1, s32[4]{0:T(128)} %sizes_hbm.1, s32[4,4]{1,0:T(4,128)} %near_hbm.1, s32[4]{0:T(128)} %count_hbm.1, s32[1,128]{1,0:T(1,128)} %mask_hbm.1), custom_call_target="tpu_custom_call" | custom-call | tf_op jit(solution)/shard_map/pallas_call | solution.py:361
  57.7 1.3 %fusion = (f32[4,128]{1,0:T(4,128)}, f32[4,128]{1,0:T(4,128)}) fusion(f32[8,128]{1,0:T(8,128)} %shard_map.95), kind=kLoop, calls=%fused_computation | loop fusion | bytes 8192 | tf_op jit(solution)/shard_map/slice | solution.py:400

commit v4 on v3

--- a/solution.py
+++ b/solution.py
@@ -13,8 +13,8 @@
 spread_sq = 0.25
 norm_eps = 1e-06
 
-HALO_ONE, HALO_TWO, COEF, SKEL, FAR_ONE, FAR_TWO, SKY_ONE, SKY_TWO, MIX_PART, MIX_ALL, SUMS = range(11)
-EXCHANGES = 11
+HALO_ONE, HALO_TWO, COEF, SKEL, SKEL_PAIR, FAR_ONE, FAR_TWO, SKY_ONE, SKY_TWO, MIX_PART, MIX_ALL, SUMS = range(12)
+EXCHANGES = 12
 
 
 def hops(step):
@@ -54,6 +54,7 @@
     core, z, x, yl = lax.rem(g, 2), lax.rem(g // 2, 8), lax.rem(g // 16, 4), g // 64
     low = {(dz, dc): lax.rem(z + dz, 8) * 2 + lax.rem(core + dc, 2) for dz in range(8) for dc in range(2)}
     high = {(dx, dy): lax.rem(yl + dy, 2) * 64 + lax.rem(x + dx, 4) * 16 for dx in range(4) for dy in range(2)}
+    me = core * 64 + g // 2
     others = [high[s[0], s[1]] + low[s[2], s[3]] for s in OTHERS]
     tiles = [lax.rem(t + d, 4) for d in (2, 1, 3)]
     left, right = lax.rem(g + 127, 128), lax.rem(g + 1, 128)
@@ -103,8 +104,24 @@
     sk_lo = jnp.concatenate([skel_ref[c, :, :128] for c in range(3)], axis=0)
     sk_hi = jnp.concatenate([skel_ref[c, :, 128:] for c in range(3)], axis=0)
     goals = jnp.where(goal_half == 0, sk_lo, sk_hi)
-    skb[g, 0:3] = jnp.where(own_half == 0, sk_lo, sk_hi)
-
+    skb[me, 0:3] = jnp.where(own_half == 0, sk_lo, sk_hi)
+
+    points_of = basis_ref[...].reshape(512, 256)
+    masked = points_of * live_col[...].reshape(512, 128)[:, 0:1]
+
+    def product(left, right):
+        return lax.dot_general(
+            left, right, (((0,), (0,)), ((), ())), precision=lax.Precision.HIGHEST, preferred_element_type=f32
+        )
+
+    upper = product(masked[:, :128], points_of)
+    lower = product(masked[:, 128:], points_of[:, 128:])
+    mix_own[0] = upper[0:96, :128]
+    mix_own[1, 0:32] = upper[96:128, :128]
+    mix_own[1, 32:96] = upper[0:64, 128:]
+    mix_own[2, 0:64] = upper[64:128, 128:]
+    mix_own[2, 64:96] = lower[0:32]
+    mix_own[3] = lower[32:128]
     pl.semaphore_wait(barrier, 127 + 9)
 
     def send(src, dst, which, dev):
@@ -153,7 +170,7 @@
                     acc = acc + values * (source * weight)
                 return acc
 
-            acc = lax.fori_loop(0, 4, body, jnp.zeros((128, 128), f32), unroll=2)
+            acc = lax.fori_loop(0, 4, body, jnp.zeros((128, 128), f32), unroll=4)
             ucol[a] = live_col[a] * (field[a] + jnp.sum(acc, axis=1, keepdims=True))
 
     def near_first():
@@ -168,12 +185,12 @@
     def near_second():
         near_apply(acol, lambda a, slot, tt, place, leaf: (gnear[a * 16 + slot * 4 + tt], hal2[place, leaf]))
 
-    def far_values():
+    def far_values(side):
         def body(b, carry):
-            gfar[b] = kernel_values(tfar, 0, skb[b])
+            gfar[2 * b + side] = kernel_values(tfar, 0, skb[64 * side + b])
             return carry
 
-        lax.fori_loop(0, 128, body, 0, unroll=4)
+        lax.fori_loop(0, 64, body, 0, unroll=4)
 
     def far_apply(n):
         def body(b, acc):
@@ -224,28 +241,13 @@
 
     to_tiles(abuf, COEF)
     to_halo(hal1, HALO_ONE)
-
-    points_of = basis_ref[...].reshape(512, 256)
-    masked = points_of * live_col[...].reshape(512, 128)[:, 0:1]
-
-    def product(left, right):
-        return lax.dot_general(
-            left, right, (((0,), (0,)), ((), ())), precision=lax.Precision.HIGHEST, preferred_element_type=f32
-        )
-
-    upper = product(masked[:, :128], points_of)
-    lower = product(masked[:, 128:], points_of[:, 128:])
-    mix_own[0] = upper[0:96, :128]
-    mix_own[1, 0:32] = upper[96:128, :128]
-    mix_own[1, 32:96] = upper[0:64, 128:]
-    mix_own[2, 0:64] = upper[64:128, 128:]
-    mix_own[2, 64:96] = lower[0:32]
-    mix_own[3] = lower[32:128]
+    for step, gg in zip(OTHERS, others):
+        if step[3] == 0:
+            send(skb.at[me, pl.ds(0, 3)], skb.at[me, pl.ds(0, 3)], SKEL, (gg, t))
     for tt in tiles:
         send(mix_own.at[tt], mix_part.at[t], MIX_PART, (g, tt))
     mix_part[t] = mix_own[t]
-    for gg in others:
-        send(skb.at[g, pl.ds(0, 3)], skb.at[g, pl.ds(0, 3)], SKEL, (gg, t))
+
     goal_rows = [goals[c : c + 1] for c in range(3)]
     cols = columns(
         [-2.0 * pts_ref[c] for c in range(3)] + [sum(pts_ref[c] * pts_ref[c] for c in range(3))]
@@ -263,12 +265,16 @@
     to_others(cbuf.at[0], FAR_ONE)
     wait(hal1.at[pl.ds(0, 11)], HALO_ONE)
     near_first()
+    wait(skb.at[pl.ds(0, 63), pl.ds(0, 3)], SKEL)
+    half = skb.at[pl.ds(core * 64, 64), pl.ds(0, 3)]
+    send(half, half, SKEL_PAIR, (g + 1 - 2 * core, t))
     wait(mix_part.at[pl.ds(0, 3)], MIX_PART)
     mix_all[t] = mix_part[0] + mix_part[1] + mix_part[2] + mix_part[3]
     to_tiles(mix_all, MIX_ALL)
     near_parts(0, [scol])
-    wait(skb.at[pl.ds(0, 127), pl.ds(0, 3)], SKEL)
-    far_values()
+    far_values(core)
+    wait(skb.at[pl.ds(0, 64), pl.ds(0, 3)], SKEL_PAIR)
+    far_values(1 - core)
     wait(cbuf.at[0, pl.ds(0, 127)], FAR_ONE)
     pbuf[0, t, 0:1] = far_apply(0)
     to_tiles(pbuf.at[0], SKY_ONE)
@@ -347,7 +353,8 @@
     drain(abuf.at[pl.ds(0, 3)], COEF)
     drain(mix_part.at[pl.ds(0, 3)], MIX_PART)
     drain(mix_all.at[pl.ds(0, 3)], MIX_ALL)
-    drain(skb.at[pl.ds(0, 127), pl.ds(0, 3)], SKEL)
+    drain(skb.at[pl.ds(0, 63), pl.ds(0, 3)], SKEL)
+    drain(skb.at[pl.ds(0, 64), pl.ds(0, 3)], SKEL_PAIR)
     drain(cbuf.at[0, pl.ds(0, 127)], FAR_ONE)
     drain(cbuf.at[1, pl.ds(0, 127)], FAR_TWO)
     drain(pbuf.at[0, pl.ds(0, 3)], SKY_ONE)

time: 59.2 us -> 57.8 us (0.976)
  Pallas kernels: 57.1 us -> 55.6 us
    pallas_call x1, Pallas kernels: 57.1 us -> 55.6 us  [per_device(): pl.pallas_call(kernel, out_shape=jax.ShapeDtypeStruct((8, 128), f32), in_...]
where the time goes in v4:
time: 57.8 us; the launch traced here: 57.6 us
  Pallas kernels  55.6 us (96%)
  local copies, waits for them, and re-layouts  1.33 us (2%)
  between operations  0.64 us (1%)
    pallas_call x1, Pallas kernels, per_device(): pl.pallas_call(kernel, out_shape=jax.ShapeDtypeStruct((8, 128), f32), in_...  55.6 us
    slice x1, local copies, waits for them, and re-layouts, per_device(): return (both[0:4], both[4:8])  1.33 us

profile of v4, /device:TPU:1, one launch (start us, length us, event | category | flops | bytes accessed | tf_op | source)
XLA Modules:
  0.0 57.6 jit_solution(16972201971710167894)
XLA Ops:
  0.6 55.6 %shard_map.95 = f32[8,128]{1,0:T(8,128)} custom-call(f32[4,128]{1,0:T(4,128)} %rs_hbm.1, f32[3,4,128]{2,1,0:T(4,128)} %pts_hbm.1, f32[4,128,256]{2,1,0:T(8,128)} %basis_hbm.1, f32[3,1,256]{2,1,0:T(1,128)} %bitcast.1, s32[4]{0:T(128)} %sizes_hbm.1, s32[4,4]{1,0:T(4,128)} %near_hbm.1, s32[4]{0:T(128)} %count_hbm.1, s32[1,128]{1,0:T(1,128)} %mask_hbm.1), custom_call_target="tpu_custom_call" | custom-call | tf_op jit(solution)/shard_map/pallas_call | solution.py:368
  56.3 1.3 %fusion = (f32[4,128]{1,0:T(4,128)}, f32[4,128]{1,0:T(4,128)}) fusion(f32[8,128]{1,0:T(8,128)} %shard_map.95), kind=kLoop, calls=%fused_computation | loop fusion | bytes 8192 | tf_op jit(solution)/shard_map/slice | solution.py:407

commit v5 on v4

--- a/solution.py
+++ b/solution.py
@@ -26,6 +26,8 @@
     [(dx, dyl, dz, dc) for dx in range(4) for dyl in range(2) for dz in range(8) for dc in range(2) if dx or dyl or dz or dc],
     key=lambda step: -hops(step),
 )
+
+FAR = 12
 
 
 def kernel(
@@ -48,9 +50,6 @@
              (near_hbm, near_ref), (count_hbm, count_ref), (mask_hbm, mask_ref)]
         )
     ]
-    for load in loads:
-        load.start()
-
     core, z, x, yl = lax.rem(g, 2), lax.rem(g // 2, 8), lax.rem(g // 16, 4), g // 64
     low = {(dz, dc): lax.rem(z + dz, 8) * 2 + lax.rem(core + dc, 2) for dz in range(8) for dc in range(2)}
     high = {(dx, dy): lax.rem(yl + dy, 2) * 64 + lax.rem(x + dx, 4) * 16 for dx in range(4) for dy in range(2)}
@@ -60,10 +59,14 @@
     left, right = lax.rem(g + 127, 128), lax.rem(g + 1, 128)
 
     barrier = pltpu.get_barrier_semaphore()
+    for gg in others[:FAR]:
+        pl.semaphore_signal(barrier, inc=1, device_id=(gg, t), device_id_type=MESH)
     for tt in tiles:
         for gg in (left, right, g):
             pl.semaphore_signal(barrier, inc=1, device_id=(gg, tt), device_id_type=MESH)
-    for gg in others:
+    for load in loads:
+        load.start()
+    for gg in others[FAR:]:
         pl.semaphore_signal(barrier, inc=1, device_id=(gg, t), device_id_type=MESH)
 
     loads[0].wait()
@@ -139,8 +142,8 @@
         for tt in tiles:
             send(buf.at[t], buf.at[t], which, (g, tt))
 
-    def to_others(buf, which):
-        for gg in others:
+    def to_others(buf, which, goals=others):
+        for gg in goals:
             send(buf.at[g], buf.at[g], which, (gg, t))
 
     def to_halo(buf, which):
@@ -190,14 +193,14 @@
             gfar[2 * b + side] = kernel_values(tfar, 0, skb[64 * side + b])
             return carry
 
-        lax.fori_loop(0, 64, body, 0, unroll=4)
+        lax.fori_loop(0, 64, body, 0, unroll=8)
 
     def far_apply(n):
         def body(b, acc):
             weight = jnp.where(mask_ref[0, b] != 0, far_scale, 0.0)
             return acc + gfar[b] * (cbuf[n, b] * weight)
 
-        acc = lax.fori_loop(0, 128, body, jnp.zeros((128, 128), f32), unroll=8)
+        acc = lax.fori_loop(0, 128, body, jnp.zeros((128, 128), f32), unroll=16)
         return jnp.sum(acc.T, axis=0, keepdims=True)
 
     def near_parts(n, fields):
@@ -286,15 +289,16 @@
     mix[3] = jnp.concatenate([mix_all[2, 64:96], mix_all[3]], axis=0)
     wait(pbuf.at[0, pl.ds(0, 3)], SKY_ONE)
     sky1_lo, sky1_hi, r1_lo, r1_hi, dots1 = gathered(0)
+
+    m1_lo, m1_hi = mixed(sky1_lo, sky1_hi)
+    two_lo, two_hi = r1_lo + m1_lo, r1_hi + m1_hi
+    cbuf[1, g] = jnp.where(own_half == 0, two_lo, two_hi)
+    to_others(cbuf.at[1], FAR_TWO, others[:FAR])
     a_row = image(sky1_lo, sky1_hi, True)
-
     for a in range(4):
         hal2[4 + t, a] = a_row[a : a + 1]
     to_halo(hal2, HALO_TWO)
-    m1_lo, m1_hi = mixed(sky1_lo, sky1_hi)
-    two_lo, two_hi = r1_lo + m1_lo, r1_hi + m1_hi
-    cbuf[1, g] = jnp.where(own_half == 0, two_lo, two_hi)
-    to_others(cbuf.at[1], FAR_TWO)
+    to_others(cbuf.at[1], FAR_TWO, others[FAR:])
     wait(hal2.at[pl.ds(0, 11)], HALO_TWO)
     near_second()
     near_parts(1, [scol, acol])

time: 57.8 us -> 57.3 us (level)
  no operation moved by 1% of the time
where the time goes in v5:
time: 57.3 us; the launch traced here: 57.1 us
  Pallas kernels  55.1 us (96%)
  local copies, waits for them, and re-layouts  1.33 us (2%)
  between operations  0.64 us (1%)
    pallas_call x1, Pallas kernels, per_device(): pl.pallas_call(kernel, out_shape=jax.ShapeDtypeStruct((8, 128), f32), in_...  55.1 us
    slice x1, local copies, waits for them, and re-layouts, per_device(): return (both[0:4], both[4:8])  1.33 us

profile of v5, /device:TPU:1, one launch (start us, length us, event | category | flops | bytes accessed | tf_op | source)
XLA Modules:
  0.0 57.1 jit_solution(6504175682933634453)
XLA Ops:
  0.6 55.1 %shard_map.95 = f32[8,128]{1,0:T(8,128)} custom-call(f32[4,128]{1,0:T(4,128)} %rs_hbm.1, f32[3,4,128]{2,1,0:T(4,128)} %pts_hbm.1, f32[4,128,256]{2,1,0:T(8,128)} %basis_hbm.1, f32[3,1,256]{2,1,0:T(1,128)} %bitcast.1, s32[4]{0:T(128)} %sizes_hbm.1, s32[4,4]{1,0:T(4,128)} %near_hbm.1, s32[4]{0:T(128)} %count_hbm.1, s32[1,128]{1,0:T(1,128)} %mask_hbm.1), custom_call_target="tpu_custom_call" | custom-call | tf_op jit(solution)/shard_map/pallas_call | solution.py:372
  55.8 1.3 %fusion = (f32[4,128]{1,0:T(4,128)}, f32[4,128]{1,0:T(4,128)}) fusion(f32[8,128]{1,0:T(8,128)} %shard_map.95), kind=kLoop, calls=%fused_computation | loop fusion | bytes 8192 | tf_op jit(solution)/shard_map/slice | solution.py:411

commit v6 on v5

--- a/solution.py
+++ b/solution.py
@@ -268,13 +268,13 @@
     to_others(cbuf.at[0], FAR_ONE)
     wait(hal1.at[pl.ds(0, 11)], HALO_ONE)
     near_first()
-    wait(skb.at[pl.ds(0, 63), pl.ds(0, 3)], SKEL)
-    half = skb.at[pl.ds(core * 64, 64), pl.ds(0, 3)]
-    send(half, half, SKEL_PAIR, (g + 1 - 2 * core, t))
     wait(mix_part.at[pl.ds(0, 3)], MIX_PART)
     mix_all[t] = mix_part[0] + mix_part[1] + mix_part[2] + mix_part[3]
     to_tiles(mix_all, MIX_ALL)
     near_parts(0, [scol])
+    wait(skb.at[pl.ds(0, 63), pl.ds(0, 3)], SKEL)
+    half = skb.at[pl.ds(core * 64, 64), pl.ds(0, 3)]
+    send(half, half, SKEL_PAIR, (g + 1 - 2 * core, t))
     far_values(core)
     wait(skb.at[pl.ds(0, 64), pl.ds(0, 3)], SKEL_PAIR)
     far_values(1 - core)
@@ -328,27 +328,26 @@
     dots = jnp.sum(rblk[...], axis=0)
     ss, sa, sb, aa, ab, bb = [dots[:, i : i + 1] for i in range(6)]
 
-    beta_sq = ss + norm_eps
-    beta = jnp.sqrt(beta_sq)
-    h11 = sa / beta_sq
-    h21_sq = jnp.maximum((aa - 2.0 * h11 * sa + h11 * h11 * ss) / beta_sq, 0.0) + norm_eps
+    inv_beta_sq = 1.0 / (ss + norm_eps)
+    h11 = sa * inv_beta_sq
+    h21_sq = jnp.maximum((aa - 2.0 * h11 * sa + h11 * h11 * ss) * inv_beta_sq, 0.0) + norm_eps
     h21 = jnp.sqrt(h21_sq)
-    h12 = (sb - h11 * sa) / (beta_sq * h21)
-    h22 = (ab - h11 * aa - h11 * sb + h11 * h11 * sa) / (beta_sq * h21_sq)
-    w_sq = (bb - 2.0 * h11 * ab + h11 * h11 * aa) / (beta_sq * h21_sq)
-    first_sq = ss / beta_sq
-    second_sq = (h21_sq - norm_eps) / h21_sq
-    cross_sq = h11 * (1.0 - first_sq) / h21
+    inv_h21_sq = 1.0 / h21_sq
+    inv_h21 = h21 * inv_h21_sq
+    h12 = (sb - h11 * sa) * inv_beta_sq * inv_h21
+    h22 = (ab - h11 * aa - h11 * sb + h11 * h11 * sa) * inv_beta_sq * inv_h21_sq
+    w_sq = (bb - 2.0 * h11 * ab + h11 * h11 * aa) * inv_beta_sq * inv_h21_sq
+    first_sq = ss * inv_beta_sq
+    second_sq = (h21_sq - norm_eps) * inv_h21_sq
+    cross_sq = h11 * (norm_eps * inv_beta_sq) * inv_h21
     rest_sq = w_sq - h12 * h12 * (2.0 - first_sq) - h22 * h22 * (2.0 - second_sq) + 2.0 * h12 * h22 * cross_sq
     h32_sq = jnp.maximum(rest_sq, 0.0) + norm_eps
     m_aa = h11 * h11 + h21_sq
     m_ab = h11 * h12 + h21 * h22
     m_bb = h12 * h12 + h22 * h22 + h32_sq
-    determ = m_aa * m_bb - m_ab * m_ab
-    y_one = beta * (m_bb * h11 - m_ab * h12) / determ
-    y_two = beta * (m_aa * h12 - m_ab * h11) / determ
-    c_one = y_one / beta
-    c_two = y_two / (beta * h21)
+    inv_determ = 1.0 / (m_aa * m_bb - m_ab * m_ab)
+    c_one = (m_bb * h11 - m_ab * h12) * inv_determ
+    c_two = (m_aa * h12 - m_ab * h11) * inv_determ * inv_h21
     out_ref[0:4] = c_one * s_row + c_two * (a_row - h11 * s_row)
     out_ref[4:8] = s_row - c_one * a_row - c_two * (b_row - h11 * a_row)
 

time: 57.3 us -> 57.3 us (level)
  no operation moved by 1% of the time
where the time goes in v6:
time: 57.3 us; the launch traced here: 57.1 us
  Pallas kernels  55.2 us (96%)
  local copies, waits for them, and re-layouts  1.33 us (2%)
  between operations  0.64 us (1%)
    pallas_call x1, Pallas kernels, per_device(): pl.pallas_call(kernel, out_shape=jax.ShapeDtypeStruct((8, 128), f32), in_...  55.2 us
    slice x1, local copies, waits for them, and re-layouts, per_device(): return (both[0:4], both[4:8])  1.33 us

profile of v6, /device:TPU:1, one launch (start us, length us, event | category | flops | bytes accessed | tf_op | source)
XLA Modules:
  0.0 57.1 jit_solution(8837780960792704860)
XLA Ops:
  0.6 55.2 %shard_map.95 = f32[8,128]{1,0:T(8,128)} custom-call(f32[4,128]{1,0:T(4,128)} %rs_hbm.1, f32[3,4,128]{2,1,0:T(4,128)} %pts_hbm.1, f32[4,128,256]{2,1,0:T(8,128)} %basis_hbm.1, f32[3,1,256]{2,1,0:T(1,128)} %bitcast.1, s32[4]{0:T(128)} %sizes_hbm.1, s32[4,4]{1,0:T(4,128)} %near_hbm.1, s32[4]{0:T(128)} %count_hbm.1, s32[1,128]{1,0:T(1,128)} %mask_hbm.1), custom_call_target="tpu_custom_call" | custom-call | tf_op jit(solution)/shard_map/pallas_call | solution.py:371
  55.8 1.3 %fusion = (f32[4,128]{1,0:T(4,128)}, f32[4,128]{1,0:T(4,128)}) fusion(f32[8,128]{1,0:T(8,128)} %shard_map.95), kind=kLoop, calls=%fused_computation | loop fusion | bytes 8192 | tf_op jit(solution)/shard_map/slice | solution.py:410
